TPU v7x, 128 devices: a whole 4x4x4 slice. The times are simulated.
128 devices in a mesh: seq: 32 (over z, x, core), batch: 4 (over y).
Axes of the slice: x: 4, y: 4, z: 4, core: 2. Of those that a mesh axis runs over, the one named last changes fastest.
Arguments:
- query_rows: bfloat16 [4, 4096, 1024], P('batch', 'seq'), may hold values from -6 to 6
- key_rows: bfloat16 [4, 4096, 1024], P('batch', 'seq'), may hold values from -6 to 6
- value_rows: bfloat16 [4, 4096, 2048], P('batch', 'seq'), may hold values from -6 to 6
- gate_z: bfloat16 [4, 4096, 2048], P('batch', 'seq'), may hold values from -6 to 6
- log_decay: float32 [4, 16, 4096], P('batch', None, 'seq'), may hold values from -0.7 to 0
- write_strength: float32 [4, 16, 4096], P('batch', None, 'seq'), may hold values from 0.0005 to 0.1
- norm_gain: float32 [128], replicated, may hold values from 0.1 to 1.9
- out_weight: bfloat16 [2048, 2048], replicated, may hold values from -0.125 to 0.125
- residual: bfloat16 [4, 4096, 2048], P('batch', 'seq'), may hold values from -6 to 6
- post_gain: float32 [2048], replicated, may hold values from 0.1 to 1.9
- expert_ids: int32 [4, 4096, 10], P('batch', 'seq'), may hold values from 0 to 255, all different within a row; in each aligned block of 128 rows (0 to 127, 128 to 255, ..., all dimensions but the last counted through in order) at most 7 rows name the same one
- gate_scores: float32 [4, 4096, 10], P('batch', 'seq'), may hold values from 0.1 to 1
- expert_up: bfloat16 [256, 2048, 1024], P(('seq', 'batch')), may hold values from -0.125 to 0.125
- expert_down: bfloat16 [256, 512, 2048], P(('seq', 'batch')), may hold values from -0.25 to 0.25
Outputs:
- mixed: bfloat16 [4, 4096, 2048], P('batch', 'seq')
Inputs may be any that keep to these rules, and one draw needn't show every extreme that they name: `expert_ids`: each row names 10 different experts; among the rows of one device no expert is named by more than 7 rows, a bound that some block reaches.
All inputs are finite; a program needn't handle non-finite values.
Results may differ from a plain program's by a relative error of at most 0.005.
Values may be sent and summed in bfloat16 or wider, within the bound.
A program may use at most 256 MiB of HBM per device.

v0:
```python
import jax
import jax.numpy as jnp
from jax import lax
from jax.sharding import PartitionSpec as P

DK = 128
SPAN = 64


PRECISE = lax.Precision.HIGHEST
EPSILON = 1e-06


def carried_in(value, axis, join, neutral):
    count, mine = (lax.axis_size(axis), lax.axis_index(axis))
    pieces = jax.tree.map(lambda part: lax.all_gather(part, axis), value)
    total = jax.tree.map(
        lambda part, zero: jnp.full_like(part, 0) + jnp.asarray(zero, part.dtype), value, neutral
    )

    def turn(position, total):
        longer = join(total, jax.tree.map(lambda part: part[position], pieces))
        return jax.tree.map(lambda new, old: jnp.where(position < mine, new, old), longer, total)

    return lax.fori_loop(0, count - 1, turn, total)


def unit_rows(tensor):
    return tensor / jnp.sqrt(jnp.sum(tensor * tensor, axis=-1, keepdims=True) + EPSILON)


def block_terms(query_in, key_in, value_in, decay_in, strength_in, block, head_dim):
    head_count, length = decay_in.shape
    nblocks = length // block
    query_unit = unit_rows(
        query_in.astype(jnp.float32).reshape(length, -1, head_dim)
    ) * head_dim ** (-0.5)
    key_unit = unit_rows(key_in.astype(jnp.float32).reshape(length, -1, head_dim))
    group_size = head_count // query_unit.shape[1]
    value_full = value_in.astype(jnp.float32).reshape(length, head_count, -1)
    value_width = value_full.shape[-1]

    def split_heads(tensor):
        return jnp.transpose(tensor, (1, 0, 2)).reshape(
            head_count, nblocks, block, tensor.shape[-1]
        )

    query_blk = split_heads(jnp.repeat(query_unit, group_size, axis=1))
    key_blk = split_heads(jnp.repeat(key_unit, group_size, axis=1))
    value_blk = split_heads(value_full)
    cum_decay = jnp.cumsum(decay_in.reshape(head_count, nblocks, block), axis=-1)
    beta_block = strength_in.reshape(head_count, nblocks, block)
    decay_gap = cum_decay[..., :, None] - cum_decay[..., None, :]
    strict = jnp.tril(jnp.ones((block, block), dtype=bool), -1)
    inclusive = jnp.tril(jnp.ones((block, block), dtype=bool), 0)
    decay_strict = jnp.where(strict, jnp.exp(jnp.where(strict, decay_gap, 0.0)), 0.0)
    decay_incl = jnp.where(inclusive, jnp.exp(jnp.where(inclusive, decay_gap, 0.0)), 0.0)
    key_key = jnp.einsum("hncd,hnjd->hncj", key_blk, key_blk, precision=PRECISE)
    query_key = jnp.einsum("hncd,hnjd->hncj", query_blk, key_blk, precision=PRECISE)
    gamma = jnp.exp(cum_decay)
    system = jnp.eye(block, dtype=jnp.float32) + beta_block[..., None] * decay_strict * key_key
    rhs = jnp.concatenate(
        [beta_block[..., None] * value_blk, (beta_block * gamma)[..., None] * key_blk], axis=-1
    )
    solved = lax.linalg.triangular_solve(
        system, rhs, left_side=True, lower=True, unit_diagonal=True
    )
    write_v = solved[..., :value_width]
    write_k = solved[..., value_width:]
    tail_keys = jnp.exp(cum_decay[..., -1:] - cum_decay)[..., None] * key_blk
    ident = jnp.eye(head_dim, dtype=jnp.float32)
    trans = gamma[..., -1][..., None, None] * ident - jnp.einsum(
        "hncd,hnce->hnde", tail_keys, write_k, precision=PRECISE
    )
    inject = jnp.einsum("hncd,hnce->hnde", tail_keys, write_v, precision=PRECISE)
    scores = decay_incl * query_key
    reader = gamma[..., None] * query_blk - jnp.einsum(
        "hncj,hnjd->hncd", scores, write_k, precision=PRECISE
    )
    local = jnp.einsum("hncj,hnje->hnce", scores, write_v, precision=PRECISE)
    return (trans, inject, reader, local)


def gated_norm(retained, gate_in, norm_gain):
    length, head_count, value_width = retained.shape
    gate_full = gate_in.astype(jnp.float32).reshape(length, head_count, value_width)
    scaled = retained * lax.rsqrt(jnp.mean(retained * retained, axis=-1, keepdims=True) + EPSILON)
    normed = scaled * norm_gain * jax.nn.silu(gate_full)
    return normed.astype(jnp.bfloat16).reshape(length, head_count * value_width)


def compose(earlier, later):
    product = jnp.einsum("hde,hef->hdf", later[0], earlier[0], precision=PRECISE)
    carried = jnp.einsum("hde,hef->hdf", later[0], earlier[1], precision=PRECISE) + later[1]
    return (product, carried)


def shards(
    query_rows,
    key_rows,
    value_rows,
    gate_z,
    log_decay,
    write_strength,
    norm_gain,
    out_weight,
    residual,
    post_gain,
    expert_ids,
    gate_scores,
    expert_up,
    expert_down,
):
    tok_count = query_rows.shape[1]
    model_width = residual.shape[2]
    trans, inject, reader, local = block_terms(
        query_rows[0], key_rows[0], value_rows[0], log_decay[0], write_strength[0], SPAN, DK
    )
    head_count = trans.shape[0]
    ident = jnp.broadcast_to(
        jnp.eye(trans.shape[-1], dtype=jnp.float32), (head_count, trans.shape[-1], trans.shape[-1])
    )
    begin_pair = (ident, jnp.zeros((head_count, inject.shape[2], inject.shape[3]), jnp.float32))

    def advance_block(carry, block_items):
        product, carried = carry
        step_trans, step_inject, step_reader, step_local = block_items
        reach_back = jnp.einsum("hcd,hde->hce", step_reader, product, precision=PRECISE)
        partial_out = (
            jnp.einsum("hcd,hde->hce", step_reader, carried, precision=PRECISE) + step_local
        )
        product = jnp.einsum("hde,hef->hdf", step_trans, product, precision=PRECISE)
        carried = jnp.einsum("hde,hef->hdf", step_trans, carried, precision=PRECISE) + step_inject
        return ((product, carried), (reach_back, partial_out))

    block_items = tuple((jnp.moveaxis(tensor, 1, 0) for tensor in (trans, inject, reader, local)))
    (whole_trans, whole_inject), (reach_back, partial_out) = lax.scan(
        advance_block, begin_pair, block_items
    )
    prefix_pair = carried_in((whole_trans, whole_inject), "seq", compose, begin_pair)
    incoming = prefix_pair[1]
    blocks_out = partial_out + jnp.einsum("nhcd,hde->nhce", reach_back, incoming, precision=PRECISE)
    retained = (
        jnp.transpose(blocks_out, (1, 0, 2, 3))
        .reshape(head_count, tok_count, -1)
        .transpose(1, 0, 2)
    )
    normed = gated_norm(retained, gate_z[0], norm_gain)
    mid = residual[0].astype(jnp.float32) + jnp.dot(
        normed, out_weight, preferred_element_type=jnp.float32
    )
    moe_in = (
        mid * lax.rsqrt(jnp.mean(mid * mid, axis=-1, keepdims=True) + EPSILON) * post_gain
    ).astype(jnp.bfloat16)
    scores = gate_scores[0]
    weights = scores / jnp.sum(scores, axis=-1, keepdims=True)
    expert_row = expert_ids[0]
    top_count = expert_row.shape[-1]
    seq_count = lax.axis_size("seq")
    batch_count = lax.axis_size("batch")
    device_count = seq_count * batch_count
    exp_dev = expert_up.shape[0]
    total_experts = exp_dev * device_count
    capacity = max(2, (5 * tok_count * top_count + 4 * total_experts - 1) // (4 * total_experts))
    flat_ids = expert_row.reshape(-1)
    one_hot = (flat_ids[:, None] == jnp.arange(total_experts, dtype=jnp.int32)[None, :]).astype(
        jnp.int32
    )
    rank_in = jnp.take_along_axis(jnp.cumsum(one_hot, axis=0), flat_ids[:, None], axis=1)[:, 0] - 1
    slot_index = (
        flat_ids % exp_dev * (device_count * capacity) + flat_ids // exp_dev * capacity + rank_in
    )
    owner = (
        jnp.full((exp_dev * device_count * capacity,), tok_count, jnp.int32)
        .at[slot_index]
        .set(jnp.arange(tok_count * top_count, dtype=jnp.int32) // top_count)
    )
    padded = jnp.concatenate([moe_in, jnp.zeros((1, model_width), jnp.bfloat16)], axis=0)
    outgoing = padded[owner].reshape(exp_dev, device_count, capacity, model_width)
    ffe_width = expert_down.shape[1]
    arrived = lax.all_to_all(outgoing, ("seq", "batch"), split_axis=1, concat_axis=1, tiled=True)
    shaped = arrived.reshape(exp_dev, -1, model_width)
    both = jnp.einsum("jrd,jdf->jrf", shaped, expert_up, preferred_element_type=jnp.float32)
    hidden = (jax.nn.silu(both[..., :ffe_width]) * both[..., ffe_width:]).astype(jnp.bfloat16)
    result = jnp.einsum(
        "jrf,jfd->jrd", hidden, expert_down, preferred_element_type=jnp.float32
    ).astype(jnp.bfloat16)
    send_result = result.reshape(arrived.shape)
    returned = lax.all_to_all(
        send_result, ("seq", "batch"), split_axis=1, concat_axis=1, tiled=True
    )
    picked = returned.reshape(-1, model_width)[slot_index].reshape(
        tok_count, top_count, model_width
    )
    mixed = mid + jnp.einsum("tk,tkd->td", weights, picked.astype(jnp.float32), precision=PRECISE)
    return mixed.astype(jnp.bfloat16)[None]


def solution(mesh):
    return jax.shard_map(
        shards,
        mesh=mesh,
        in_specs=(
            P("batch", "seq", None),
            P("batch", "seq", None),
            P("batch", "seq", None),
            P("batch", "seq", None),
            P("batch", None, "seq"),
            P("batch", None, "seq"),
            P(),
            P(),
            P("batch", "seq", None),
            P(),
            P("batch", "seq", None),
            P("batch", "seq", None),
            P(("seq", "batch"), None, None),
            P(("seq", "batch"), None, None),
        ),
        out_specs=P("batch", "seq", None),
        check_vma=False,
    )
```

profile of v0, /device:TPU:1, one launch (start us, length us, event | category | flops | bytes accessed | tf_op | source)
XLA Modules:
  0.0 872.2 jit_solution(8231253379021905519)
XLA Ops:
  14.5 159.2 %custom-call.3 = f32[16,2,1,64,64]{3,4,2,1,0:T(8,128)} custom-call(f32[16,2,1,64,64]{4,3,2,1,0:T(8,128)} %fusion.48), custom_call_target="InvertDiagBlocksLowerTriangular" | custom-call | tf_op jit(solution)/shard_map/triangular_solve | solution.py:65
  183.5 5.1 convolution_bitcast_fusion.1
  188.7 5.3 bitcast_subtract_fusion
  194.1 20.0 %while.31 = (s32[]{:T(128)}, f32[16,128,128]{2,1,0:T(8,128)S(1)}, f32[16,128,128]{2,1,0:T(8,128)}, f32[2,16,64,128]{3,2,0,1:T(8,128)}, f32[2,16,64,128]{3,2,0,1:...) while((s32[]{:T(128)}, f32[16,128,128]{2,1,0:T(8,128)S(1)}, ...), condition=%wide.region_4.5_spmd.clone, body=%wide.region_3.4_spmd.clone.sunk | while | flops 1208877056 | bytes 37227752 | solution.py:137
  223.0 10.2 %gather_fusion.2 = s32[1280]{0:T(1024)S(1)} fusion(s32[1280,256]{0,1:T(8,128)S(1)} %bitcast.172, s32[1280]{0:T(1024)S(1)} %fusion.85), kind=kCustom, calls=%fused_computation.2 | custom fusion | bytes 20480 | tf_op jit(solution)/shard_map/jit(take_along_axis)/gather | solution.py:169
  233.3 5.5 scatter_custom_fusion
  238.8 94.0 %all-gather.5.cloned.1.call-done = f32[512,128,128]{2,1,0:T(8,128)} async-done(((f32[16,128,128]{2,1,0:T(8,128)}), f32[512,128,128]{2,1,0:T(8,128)}) %all-gather.5.cloned.1.call-update) | async-done | bytes 33554448 | tf_op jit(solution)/shard_map/all_gather | solution.py:16
  332.8 115.5 %all-gather.7.cloned.1.call-done = f32[512,128,128]{2,1,0:T(8,128)} async-done(((f32[16,128,128]{2,1,0:T(8,128)}), f32[512,128,128]{2,1,0:T(8,128)}) %all-gather.7.cloned.1.call-update) | async-done | bytes 33554448 | tf_op jit(solution)/shard_map/all_gather | solution.py:16
  448.3 91.0 %while.32 = (s32[]{:T(128)}, f32[16,128,128]{2,1,0:T(8,128)S(1)}, s32[]{:T(128)}, f32[32,16,128,128]{3,2,1,0:T(8,128)}, f32[32,16,128,128]{3,2,1,0:T(8,128)}, /*index=5*/s32[]{:T(128)}, s32[]{:T(128)}) while((s32[]{:T(128)}, f32[16,128,128]{2,1,0:T(8,128)S(1)}, s32[]{:T(128)}, f32[32,16,128,128]{3,2,1,0:T(8,128)}, ...), condition=%wide.region_6.7_spmd.clone, body=%wide.region_5.6_spmd.clone.sunk | while | flops 403701760 | bytes 7342687 | solution.py:25
  543.4 4.8 multiply_reduce_fusion
  548.4 8.1 gather_fusion
  556.6 11.3 %reshape.394 = bf16[2,128,7,2048]{3,2,1,0:T(8,128)(2,1)} reshape(bf16[1792,2048]{1,0:T(8,128)(2,1)} %gather_fusion) | data formatting | bytes 14680064 | tf_op jit(solution)/shard_map/reshape | solution.py:179
  567.8 15.7 %copy.92 = bf16[2,128,7,2048]{3,0,2,1:T(2,128)(2,1)S(1)} copy(bf16[2,128,7,2048]{3,2,1,0:T(8,128)(2,1)} %reshape.394) | data formatting | bytes 14680064 | tf_op jit(solution)/shard_map/reshape | solution.py:179
  583.6 94.0 %all_to_all.10 = bf16[2,128,7,2048]{3,0,2,1:T(2,128)(2,1)S(1)} all-to-all(bf16[2,128,7,2048]{3,0,2,1:T(2,128)(2,1)S(1)} %copy.92), channel_id=1, replica_groups=mesh['seq'=32,'batch'=4] {'seq','batch'}, dimensions={1} | all-to-all | bytes 14680064 | tf_op jit(solution)/shard_map/all_to_all | solution.py:181
  677.6 13.4 %fusion.32 = f32[2,896,1024]{2,1,0:T(8,128)} fusion(bf16[2,2048,1024]{2,1,0:T(8,128)(2,1)} %param.30, bf16[2,896,2048]{2,0,1:T(2,128)(2,1)S(1)} %bitcast.181), kind=kOutput, calls=%fused_computation.40 | convolution fusion | flops 7516192768 | bytes 23068672 | tf_op jit(solution)/shard_map/jrd,jdf->jrf/dot_general | solution.py:183
  691.0 8.4 convolution_convert_fusion
  699.4 21.9 %copy.94 = bf16[2,896,2048]{2,0,1:T(2,128)(2,1)} copy(bf16[2,896,2048]{2,1,0:T(8,128)(2,1)S(1)} %convolution_convert_fusion) | data formatting | bytes 14680064 | tf_op jit(solution)/shard_map/convert_element_type | solution.py:187
  721.3 5.2 all-to-all-start.1
  726.7 86.5 %all-to-all-done.1 = bf16[2,128,7,2048]{3,0,2,1:T(2,128)(2,1)} async-done(((bf16[2,128,7,2048]{3,0,2,1:T(2,128)(2,1)}), bf16[2,128,7,2048]{3,0,2,1:T(2,128)(2,1)}, u32[]{:S(2)}, u32[]{:S(2)}) %all-to-all-start.1) | async-done | bytes 7340064 | tf_op jit(solution)/shard_map/all_to_all | solution.py:189
  813.2 9.8 %copy.95 = bf16[2,128,7,2048]{3,2,1,0:T(8,128)(2,1)} copy(bf16[2,128,7,2048]{3,0,2,1:T(2,128)(2,1)} %all-to-all-done.1) | data formatting | bytes 14680064 | tf_op jit(solution)/shard_map/all_to_all | solution.py:189
  823.0 10.7 %reshape.397 = bf16[1792,2048]{1,0:T(8,128)(2,1)} reshape(bf16[2,128,7,2048]{3,2,1,0:T(8,128)(2,1)} %copy.95) | data formatting | bytes 14680064 | tf_op jit(solution)/shard_map/reshape | solution.py:192
  833.7 14.9 %gather_fusion.1 = bf16[1280,2048]{1,0:T(8,128)(2,1)} fusion(bf16[1792,2048]{1,0:T(8,128)(2,1)} %reshape.397, s32[2048]{0:T(1024)S(1)} %pad_clamp_fusion), kind=kCustom, calls=%fused_computation.1 | custom fusion | bytes 10490880 | tf_op jit(solution)/shard_map/gather | solution.py:192
  848.5 9.5 %reshape.398 = bf16[128,10,2048]{2,1,0:T(8,128)(2,1)} reshape(bf16[1280,2048]{1,0:T(8,128)(2,1)} %gather_fusion.1) | data formatting | bytes 10485760 | tf_op jit(solution)/shard_map/reshape | solution.py:192
  858.1 5.9 fusion.90
  (194 shorter events, 141.8 us)
Async XLA Ops:
  6.5 4.3 copy-start.8
  6.5 326.3 %all-gather.5.cloned.1.call-start = ((), (), s32[]{:S(2)}) async-start(), calls=%async_computation.2 | async-start | bytes 34603008 | tf_op jit(solution)/shard_map/all_gather | solution.py:16
  11.1 162.5 %copy-start.10 = (bf16[1,128,1024]{2,1,0:T(8,128)(2,1)S(1)}, bf16[1,128,1024]{2,1,0:T(8,128)(2,1)}, u32[]{:S(2)}) copy-start(bf16[1,128,1024]{2,1,0:T(8,128)(2,1)} %param.18) | copy-start | bytes 786436
  174.4 2.5 copy-start.5
  179.0 4.6 copy-start.3
  194.1 21.8 %copy-start.13 = (s32[1,128,10]{1,0,2:T(1,128)S(1)}, s32[1,128,10]{1,0,2:T(1,128)}, u32[]{:S(2)}) copy-start(s32[1,128,10]{1,0,2:T(1,128)} %param.28) | copy-start | bytes 15364
  194.1 4.4 copy-start.2
  198.5 2.3 copy-start.1
  198.5 2.3 copy-start.6
  201.9 1.0 copy-start.7
  204.1 4.5 copy-start.2
  208.5 2.3 copy-start.1
  208.5 2.3 copy-start.6
  211.9 1.0 copy-start.7
  214.1 1.0 copy-start
  215.1 233.2 %all-gather.7.cloned.1.call-start = ((), (), s32[]{:S(2)}) async-start(), calls=%async_computation.3 | async-start | bytes 34603008 | tf_op jit(solution)/shard_map/all_gather | solution.py:16
  539.3 3.2 copy-start.4
  539.3 3.2 copy-start.14
  542.4 1.0 copy-start.9
  543.4 4.8 copy-start.12
  721.3 5.3 copy-start.11
  721.3 91.9 %all-to-all-start.1 = ((bf16[2,128,7,2048]{3,0,2,1:T(2,128)(2,1)}), bf16[2,128,7,2048]{3,0,2,1:T(2,128)(2,1)}, u32[]{:S(2)}, u32[]{:S(2)}) async-start(bf16[2,128,7,2048]{3,0,2,1:T(2,128)(2,1)} %bitcast.173), calls=%async_computation.1 | async-start | bytes 14680064 | tf_op jit(solution)/shard_map/all_to_all | solution.py:189
Sparse Core Ops, SparseCore 0:
  215.2 117.5 all-gather.4
  335.1 113.1 all-gather.6
where the time goes:
time: 879 us; the launch traced here: 872 us
  waiting for transfers between devices  297 us (34%)
  other arithmetic  165 us (19%)
  matrix products  159 us (18%)
  local copies, waits for them, and re-layouts  137 us (16%)
  blocking collectives  94 us (11%)
  between operations  14.2 us (2%)
    all_gather x2, waiting for transfers between devices, carried_in(): pieces = jax.tree.map(lambda part: lax.all_gather(part, axis), value)  209 us
    another operation x4, other arithmetic, block_terms(): lax.linalg.triangular_solve(system, rhs, left_side=True, lower=True, unit...  159 us
    all_to_all x1, blocking collectives, shards(): lax.all_to_all(outgoing, ('seq', 'batch'), split_axis=1, concat_axis=1, t...  94 us
    dot_general x31, matrix products, compose(): jnp.einsum('hde,hef->hdf', later[0], earlier[1], precision=PRECISE)  87.5 us
    all_to_all x1, waiting for transfers between devices, shards(): lax.all_to_all(send_result, ('seq', 'batch'), split_axis=1, concat_axis=1...  86.5 us
    reshape x2, local copies, waits for them, and re-layouts, shards(): padded[owner].reshape(exp_dev, device_count, capacity, model_width)  27 us
    convert_element_type x1, local copies, waits for them, and re-layouts, shards(): result = jnp.einsum('jrf,jfd->jrd', hidden, expert_down, preferred_elemen...  21.9 us
    reshape x2, local copies, waits for them, and re-layouts, shards(): returned.reshape(-1, model_width)[slot_index]  20.2 us
  transfers between devices with their start and end apart: 3, of which 3 were waited for; matrix products, arithmetic and copies ran while one was open for 3% of the time, Pallas kernels for 0%

commit v1 on v0

v1 whole, which is shorter than its diff:
```python
import jax
import jax.numpy as jnp
from jax import lax
from jax.experimental import pallas as pl
from jax.experimental.pallas import tpu as pltpu
from jax.sharding import PartitionSpec as P

TOK = 128
DK = 128
HV = 16
HK = 8
GROUPS = 2
ROWS = 8
MSG = 208
EPSILON = 1e-06
PRECISE = lax.Precision.HIGHEST
F32 = jnp.float32
BF16 = jnp.bfloat16

NN = (((1,), (0,)), ((), ()))
NT = (((1,), (1,)), ((), ()))
TN = (((0,), (0,)), ((), ()))


def mul(a, b, dims=NN):
    return lax.dot_general(a, b, dims, preferred_element_type=F32)


def mul_precise(a, b, dims=NN):
    return lax.dot_general(a, b, dims, preferred_element_type=F32, precision=PRECISE)


def halves(a):
    high = a.astype(BF16)
    return high, (a - high.astype(F32)).astype(BF16)


def local_kernel(q_ref, k_ref, v_ref, ld_ref, bt_ref, msg_ref, reader_ref, local_ref, n_ref, x_ref, s_ref):
    heads = HV // GROUPS
    row = lax.broadcasted_iota(jnp.int32, (TOK, TOK), 0)
    col = lax.broadcasted_iota(jnp.int32, (TOK, TOK), 1)
    ld = ld_ref[0]
    cum_row = mul_precise(ld, (row <= col).astype(F32))
    cum_col = mul_precise((row >= col).astype(F32), ld, NT)
    beta_col = bt_ref[0].T
    units = []
    for g in range(heads // 2):
        lanes = slice(g * DK, (g + 1) * DK)
        k_raw = k_ref[:, lanes]
        q_raw = q_ref[:, lanes]
        k_full = k_raw.astype(F32)
        q_full = q_raw.astype(F32)
        k_scale = lax.rsqrt(jnp.sum(k_full * k_full, axis=-1, keepdims=True) + EPSILON)
        q_scale = lax.rsqrt(jnp.sum(q_full * q_full, axis=-1, keepdims=True) + EPSILON) * DK ** (-0.5)
        k_unit = k_full * k_scale
        k_high, k_low = halves(k_unit)
        right = jnp.concatenate([k_high, k_low], axis=1)
        key_key = mul(jnp.concatenate([k_raw, k_raw], axis=1), right, NT) * k_scale
        query_key = mul(jnp.concatenate([q_raw, q_raw], axis=1), right, NT) * q_scale
        units.append((k_unit, q_full * q_scale))
        for h in (2 * g, 2 * g + 1):
            gap = cum_col[:, h:h + 1] - cum_row[h:h + 1, :]
            decay = jnp.where(row >= col, jnp.exp(jnp.minimum(gap, 0.0)), 0.0)
            s_ref[h] = (decay * query_key).astype(BF16)
            system = jnp.where(row > col, decay * key_key, 0.0) * beta_col[:, h:h + 1]
            n_ref[h] = system
            x_ref[h] = jnp.where((row ^ col) == 1, -system, 0.0)
    for level in range(1, 7):
        cross = ((row >> level) ^ (col >> level)) == 1
        left = []
        for h in range(heads):
            part = jnp.where(cross, n_ref[h], 0.0)
            left.append(part + mul(x_ref[h].astype(BF16), part.astype(BF16)))
        for h in range(heads):
            old = x_ref[h]
            x_ref[h] = old - left[h] - mul(left[h].astype(BF16), old.astype(BF16))
    for h in range(heads):
        k_unit, q_unit = units[h // 2]
        cum = cum_col[:, h:h + 1]
        last = cum_row[h:h + 1, TOK - 1:TOK]
        beta = beta_col[:, h:h + 1]
        gamma = jnp.exp(cum)
        value = v_ref[:, h * DK:(h + 1) * DK].astype(F32) * beta
        right = jnp.concatenate([value, k_unit * (beta * gamma)], axis=1)
        write = (right + mul(x_ref[h].astype(BF16), right.astype(BF16))).astype(BF16)
        tail = (jnp.exp(last - cum) * k_unit).astype(BF16)
        moved = mul(write, tail, TN)
        trans = (-moved[DK:]).astype(BF16)
        inject = moved[:DK].astype(BF16)
        read = mul(s_ref[h], write)
        local_ref[h] = read[:, :DK]
        reader_ref[h] = (gamma * q_unit - read[:, DK:]).astype(BF16)
        whole = jnp.exp(jnp.broadcast_to(last, (16, DK)))
        part0 = whole.astype(BF16)
        part1 = (whole - part0.astype(F32)).astype(BF16)
        part2 = (whole - part0.astype(F32) - part1.astype(F32)).astype(BF16)
        line = lax.broadcasted_iota(jnp.int32, (16, DK), 0)
        parts = jnp.where(line == 0, part0.astype(F32), jnp.where(line == 1, part1.astype(F32), part2.astype(F32)))
        parts = jnp.where(line < 3, parts, 0.0).astype(BF16)
        for half in range(2):
            msg_ref[2 * h + half, 0:128] = trans
            msg_ref[2 * h + half, 128:192] = inject[half * 64:(half + 1) * 64]
            msg_ref[2 * h + half, 192:208] = parts


def local_terms(query, key, value, log_decay, strength):
    heads = HV // GROUPS
    return pl.pallas_call(
        local_kernel,
        grid=(GROUPS,),
        in_specs=[
            pl.BlockSpec((TOK, heads // 2 * DK), lambda i: (0, i)),
            pl.BlockSpec((TOK, heads // 2 * DK), lambda i: (0, i)),
            pl.BlockSpec((TOK, heads * DK), lambda i: (0, i)),
            pl.BlockSpec((1, heads, TOK), lambda i: (i, 0, 0)),
            pl.BlockSpec((1, heads, TOK), lambda i: (i, 0, 0)),
        ],
        out_specs=[
            pl.BlockSpec((2 * heads, MSG, DK), lambda i: (i, 0, 0)),
            pl.BlockSpec((heads, TOK, DK), lambda i: (i, 0, 0)),
            pl.BlockSpec((heads, TOK, DK), lambda i: (i, 0, 0)),
        ],
        out_shape=[
            jax.ShapeDtypeStruct((2 * HV, MSG, DK), BF16),
            jax.ShapeDtypeStruct((HV, TOK, DK), BF16),
            jax.ShapeDtypeStruct((HV, TOK, DK), F32),
        ],
        scratch_shapes=[
            pltpu.VMEM((heads, TOK, TOK), F32),
            pltpu.VMEM((heads, TOK, TOK), F32),
            pltpu.VMEM((heads, TOK, TOK), BF16),
        ],
        compiler_params=pltpu.CompilerParams(vmem_limit_bytes=40 << 20),
        name="local_terms",
    )(query, key, value, log_decay.reshape(GROUPS, heads, TOK), strength.reshape(GROUPS, heads, TOK))


def chain_kernel(map_ref, state_ref):
    count = map_ref.shape[0]

    def step(p, state):
        high, low = halves(state)
        state_ref[p] = high
        both = mul(jnp.concatenate([high, low], axis=0), map_ref[p, 0:128])
        parts = map_ref[p, 192:208].astype(F32)
        gamma = parts[0:1] + parts[1:2] + parts[2:3]
        return state * gamma + (both[:64] + both[64:]) + map_ref[p, 128:192].astype(F32)

    lax.fori_loop(0, count, step, jnp.zeros((64, DK), F32), unroll=4)


def chain(maps):
    count = maps.shape[0]
    return pl.pallas_call(
        chain_kernel,
        out_shape=jax.ShapeDtypeStruct((count, 64, DK), BF16),
        in_specs=[pl.BlockSpec(memory_space=pltpu.VMEM)],
        out_specs=pl.BlockSpec(memory_space=pltpu.VMEM),
        compiler_params=pltpu.CompilerParams(vmem_limit_bytes=40 << 20),
        name="chain",
    )(maps)


def finish_kernel(state_ref, reader_ref, local_ref, gate_ref, gain_ref, weight_ref, resid_ref, post_ref, mid_ref, moe_ref, normed_ref):
    step = pl.program_id(0)
    width = weight_ref.shape[1]

    @pl.when(step == 0)
    def _():
        for h in range(HV):
            kept = mul(reader_ref[h], state_ref[h], NT) + local_ref[h]
            scaled = kept * lax.rsqrt(jnp.mean(kept * kept, axis=-1, keepdims=True) + EPSILON)
            gate = gate_ref[:, h * DK:(h + 1) * DK].astype(F32)
            normed_ref[:, h * DK:(h + 1) * DK] = (
                scaled * gain_ref[...] * (gate / (1.0 + jnp.exp(-gate)))
            ).astype(BF16)

    lanes = pl.ds(pl.multiple_of(step * width, width), width)
    mid_ref[:, lanes] = resid_ref[:, lanes].astype(F32) + mul(normed_ref[...], weight_ref[...])

    @pl.when(step == pl.num_programs(0) - 1)
    def _():
        mid = mid_ref[...]
        moe_ref[...] = (
            mid * lax.rsqrt(jnp.mean(mid * mid, axis=-1, keepdims=True) + EPSILON) * post_ref[...]
        ).astype(BF16)


def finish(state, reader, local, gate, gain, weight, resid, post):
    depth, width = weight.shape
    tile = 512
    whole2 = lambda i: (0, 0)
    whole3 = lambda i: (0, 0, 0)
    return pl.pallas_call(
        finish_kernel,
        grid=(width // tile,),
        in_specs=[
            pl.BlockSpec((HV, DK, DK), whole3),
            pl.BlockSpec((HV, TOK, DK), whole3),
            pl.BlockSpec((HV, TOK, DK), whole3),
            pl.BlockSpec((TOK, HV * DK), whole2),
            pl.BlockSpec((1, DK), whole2),
            pl.BlockSpec((depth, tile), lambda i: (0, i)),
            pl.BlockSpec((TOK, width), whole2),
            pl.BlockSpec((1, width), whole2),
        ],
        out_specs=[pl.BlockSpec((TOK, width), whole2), pl.BlockSpec((TOK, width), whole2)],
        out_shape=[jax.ShapeDtypeStruct((TOK, width), F32), jax.ShapeDtypeStruct((TOK, width), BF16)],
        scratch_shapes=[pltpu.VMEM((TOK, HV * DK), BF16)],
        compiler_params=pltpu.CompilerParams(vmem_limit_bytes=40 << 20),
        name="finish",
    )(state, reader, local, gate, gain[None], weight, resid, post[None])


def expert_kernel(x_ref, up_ref, down_ref, y_ref):
    sources, _, width = x_ref.shape
    hidden_width = down_ref.shape[1]
    rows = sources * ROWS
    x = x_ref[...].astype(F32)
    results = []
    for j in range(2):
        mine = x[:, j * ROWS:(j + 1) * ROWS].reshape(rows, width).astype(BF16)
        gate = mul(mine, up_ref[j, :, :hidden_width])
        lift = mul(mine, up_ref[j, :, hidden_width:])
        hidden = (gate / (1.0 + jnp.exp(-gate)) * lift).astype(BF16)
        results.append(mul(hidden, down_ref[j]).reshape(sources, ROWS, width))
    y_ref[...] = jnp.concatenate(results, axis=1).astype(BF16)


def experts(x, up, down):
    count, rows, width = x.shape
    tile = 32
    whole3 = lambda i: (0, 0, 0)
    return pl.pallas_call(
        expert_kernel,
        grid=(count // tile,),
        in_specs=[
            pl.BlockSpec((tile, rows, width), lambda i: (i, 0, 0)),
            pl.BlockSpec(up.shape, whole3, pipeline_mode=pl.Buffered(1)),
            pl.BlockSpec(down.shape, whole3, pipeline_mode=pl.Buffered(1)),
        ],
        out_specs=pl.BlockSpec((tile, rows, width), lambda i: (i, 0, 0)),
        out_shape=jax.ShapeDtypeStruct(x.shape, BF16),
        compiler_params=pltpu.CompilerParams(vmem_limit_bytes=56 << 20),
        name="experts",
    )(x, up, down)


def shards(
    query_rows,
    key_rows,
    value_rows,
    gate_z,
    log_decay,
    write_strength,
    norm_gain,
    out_weight,
    residual,
    post_gain,
    expert_ids,
    gate_scores,
    expert_up,
    expert_down,
):
    width = residual.shape[2]
    devices = lax.axis_size("seq") * lax.axis_size("batch")
    exp_dev = expert_up.shape[0]
    total_experts = exp_dev * devices
    slots = total_experts * ROWS

    maps, reader, local = local_terms(
        query_rows[0], key_rows[0], value_rows[0], log_decay[0], write_strength[0]
    )
    maps = lax.all_to_all(maps, "seq", split_axis=0, concat_axis=0, tiled=True)
    states = chain(maps)
    states = lax.all_to_all(states, "seq", split_axis=0, concat_axis=0, tiled=True)
    mid, moe_in = finish(
        states.reshape(HV, DK, DK), reader, local, gate_z[0], norm_gain, out_weight, residual[0], post_gain
    )

    ids = expert_ids[0]
    scores = gate_scores[0]
    weights = scores / jnp.sum(scores, axis=-1, keepdims=True)
    named = ids.T[:, None, :] == jnp.arange(total_experts, dtype=jnp.int32)[None, :, None]
    chosen = jnp.sum(named.astype(F32), axis=0)
    share = jnp.sum(jnp.where(named, weights.T[:, None, :], 0.0), axis=0)
    earlier = jnp.triu(jnp.ones((TOK, TOK), BF16), 1)
    rank = jnp.dot(chosen.astype(BF16), earlier, preferred_element_type=F32)
    place = jnp.where(chosen > 0, rank, -1.0)
    pick = place[:, None, :] == jnp.arange(ROWS, dtype=F32)[None, :, None]
    take = pick.astype(BF16).reshape(slots, TOK)
    give = jnp.where(pick, share[:, None, :], 0.0).reshape(slots, TOK)
    give_high = give.astype(BF16)
    give_low = (give - give_high.astype(F32)).astype(BF16)

    outgoing = jnp.dot(take, moe_in, preferred_element_type=F32).astype(BF16)
    arrived = lax.all_to_all(
        outgoing.reshape(devices, exp_dev * ROWS, width), ("seq", "batch"), split_axis=0, concat_axis=0, tiled=True
    )
    result = experts(arrived, expert_up, expert_down)
    returned = lax.all_to_all(result, ("seq", "batch"), split_axis=0, concat_axis=0, tiled=True)
    returned = returned.reshape(slots, width)
    mixed = mid + (mul(give_high, returned, TN) + mul(give_low, returned, TN))
    return mixed.astype(BF16)[None]


def solution(mesh):
    return jax.shard_map(
        shards,
        mesh=mesh,
        in_specs=(
            P("batch", "seq", None),
            P("batch", "seq", None),
            P("batch", "seq", None),
            P("batch", "seq", None),
            P("batch", None, "seq"),
            P("batch", None, "seq"),
            P(),
            P(),
            P("batch", "seq", None),
            P(),
            P("batch", "seq", None),
            P("batch", "seq", None),
            P(("seq", "batch"), None, None),
            P(("seq", "batch"), None, None),
        ),
        out_specs=P("batch", "seq", None),
        check_vma=False,
    )
```

time: 879 us -> 312 us (0.35)
  waiting for transfers between devices: 297 us -> 32.5 us
  other arithmetic: 165 us -> 1.65 us
  matrix products: 159 us -> 5.95 us
  local copies, waits for them, and re-layouts: 137 us -> 11.5 us
  blocking collectives: 94 us -> 206 us
  Pallas kernels: 0 us -> 38.4 us
  between operations: 14.2 us -> 0.08 us
  starting transfers between devices: 5.29 us -> 15.1 us
    all_gather x2 -> x0, waiting for transfers between devices: 209 us -> none  [carried_in(): pieces = jax.tree.map(lambda part: lax.all_gather(part, axis), value)]
    another operation x10 -> x0, other arithmetic: 160 us -> none  [the longest x4 159 us: block_terms(): lax.linalg.triangular_solve(system, rhs, left_side=True, lower=True, unit...]
    dot_general x50 -> x4, matrix products: 157 us -> 5.95 us  [the longest x2 3.43 us: mul(): return lax.dot_general(a, b, dims, preferred_element_type=F32)]
    all_to_all x1 -> x2, blocking collectives: 94 us -> 206 us  [the longest x1 104 us: shards(): lax.all_to_all(outgoing.reshape(devices, exp_dev * ROWS, width), ('seq',...]
    all_to_all x1 -> x2, waiting for transfers between devices: 86.5 us -> 32.5 us  [the longest x1 22 us: shards(): maps = lax.all_to_all(maps, 'seq', split_axis=0, concat_axis=0, tiled=True)]
    reshape x6 -> x0, local copies, waits for them, and re-layouts: 47.9 us -> none  [the longest x2 27 us: shards(): padded[owner].reshape(exp_dev, device_count, capacity, model_width)]
    pallas_call x0 -> x4, Pallas kernels: none -> 38.4 us  [the longest x1 20.9 us: experts(): pl.pallas_call(expert_kernel, grid=(count // tile,), in_specs=[pl.BlockSp...]
    gather x3 -> x0, local copies, waits for them, and re-layouts: 33.2 us -> none  [the longest x1 14.9 us: shards(): returned.reshape(-1, model_width)[slot_index]]
  transfers between devices with their start and end apart: 3 -> 2, of which waited for: 3 -> 2; matrix products, arithmetic and copies ran while one was open for 3% -> 1% of each run, Pallas kernels for 0% -> 0%
where the time goes in v1:
time: 312 us
  blocking collectives  206 us (66%)
  Pallas kernels  38.4 us (12%)
  waiting for transfers between devices  32.5 us (10%)
  starting transfers between devices  15.1 us (5%)
  local copies, waits for them, and re-layouts  11.5 us (4%)
  matrix products  5.95 us (2%)
    all_to_all x1, blocking collectives, shards(): lax.all_to_all(outgoing.reshape(devices, exp_dev * ROWS, width), ('seq',...  104 us
    all_to_all x1, blocking collectives, shards(): lax.all_to_all(result, ('seq', 'batch'), split_axis=0, concat_axis=0, til...  102 us
    all_to_all x1, waiting for transfers between devices, shards(): maps = lax.all_to_all(maps, 'seq', split_axis=0, concat_axis=0, tiled=True)  22 us
    pallas_call x1, Pallas kernels, experts(): pl.pallas_call(expert_kernel, grid=(count // tile,), in_specs=[pl.BlockSp...  20.9 us
    unnamed x25, local copies, waits for them, and re-layouts  11.4 us
    all_to_all x1, waiting for transfers between devices, shards(): lax.all_to_all(states, 'seq', split_axis=0, concat_axis=0, tiled=True)  10.6 us
    all_to_all x1, starting transfers between devices, shards(): maps = lax.all_to_all(maps, 'seq', split_axis=0, concat_axis=0, tiled=True)  9.43 us
    pallas_call x1, Pallas kernels, local_terms(): pl.pallas_call(local_kernel, grid=(GROUPS,), in_specs=[pl.BlockSpec((TOK,...  9.01 us
  transfers between devices with their start and end apart: 2, of which 2 were waited for; matrix products, arithmetic and copies ran while one was open for 1% of the time, Pallas kernels for 0%

profile of v1, /device:TPU:1, one launch (start us, length us, event | category | flops | bytes accessed | tf_op | source)
XLA Modules:
  0.0 311.6 jit_solution(12758778013659549950)
XLA Ops:
  0.0 1.1 copy-done.5
  1.1 0.9 copy-done.6
  2.1 0.9 copy-done.7
  3.0 0.7 copy-done.8
  3.7 0.7 copy-done.9
  4.4 9.0 %local_terms.1 = (bf16[32,208,128]{2,1,0:T(8,128)(2,1)}, bf16[16,128,128]{2,1,0:T(8,128)(2,1)S(1)}, f32[16,128,128]{2,1,0:T(8,128)S(1)}) custom-call(bf16[128,1024]{1,0:T(8,128)(2,1)S(1)} %bitcast.41, bf16[128,1024]{1,0:T(8,128)(2,1)S(1)} %bitcast.42, bf16[128,2048]{1,0:T(8,128)(2,1)S(1)} %bitcast.40, f32[2,8,128]{2,1,0:T(8,128)S(1)} %bitcast.43, ...), custom_call_target="tpu_custom_call" | custom-call | tf_op jit(solution)/shard_map/local_terms/pallas_call | solution.py:108
  13.4 0.8 copy-done.3
  14.2 9.4 %all-to-all-start = ((bf16[32,208,128]{2,1,0:T(8,128)(2,1)}), bf16[32,208,128]{2,1,0:T(8,128)(2,1)S(1)}, u32[]{:S(2)}, u32[]{:S(2)}) async-start(bf16[32,208,128]{2,1,0:T(8,128)(2,1)} %get-tuple-element.10), calls=%async_computation | async-start | bytes 3407872 | tf_op jit(solution)/shard_map/all_to_all | solution.py:274
  24.5 0.7 reduce_sum.28
  25.2 22.0 %all-to-all-done.map_ref = bf16[32,208,128]{2,1,0:T(8,128)(2,1)S(1)} async-done(((bf16[32,208,128]{2,1,0:T(8,128)(2,1)}), bf16[32,208,128]{2,1,0:T(8,128)(2,1)S(1)}, u32[]{:S(2)}, u32[]{:S(2)}) %all-to-all-start) | async-done | bytes 1703968 | tf_op jit(solution)/shard_map/all_to_all | solution.py:274
  47.2 4.9 %chain.1 = bf16[32,64,128]{2,1,0:T(8,128)(2,1)} custom-call(bf16[32,208,128]{2,1,0:T(8,128)(2,1)S(1)} %all-to-all-done.map_ref), custom_call_target="tpu_custom_call" | custom-call | tf_op jit(solution)/shard_map/chain/pallas_call | solution.py:154
  52.1 5.7 %all-to-all-start.1 = ((bf16[32,64,128]{2,1,0:T(8,128)(2,1)}), bf16[32,64,128]{2,1,0:T(8,128)(2,1)S(1)}, u32[]{:S(2)}, u32[]{:S(2)}) async-start(bf16[32,64,128]{2,1,0:T(8,128)(2,1)} %chain.1), calls=%async_computation.1 | async-start | bytes 1048576 | tf_op jit(solution)/shard_map/all_to_all | solution.py:276
  57.8 0.7 fusion.22
  58.9 10.6 %all-to-all-done.1 = bf16[32,64,128]{2,1,0:T(8,128)(2,1)S(1)} async-done(((bf16[32,64,128]{2,1,0:T(8,128)(2,1)}), bf16[32,64,128]{2,1,0:T(8,128)(2,1)S(1)}, u32[]{:S(2)}, u32[]{:S(2)}) %all-to-all-start.1) | async-done | bytes 524320 | tf_op jit(solution)/shard_map/all_to_all | solution.py:276
  69.5 3.4 %copy-done = bf16[2048,2048]{1,0:T(8,128)(2,1)S(1)} copy-done((bf16[2048,2048]{1,0:T(8,128)(2,1)S(1)}, bf16[2048,2048]{1,0:T(8,128)(2,1)}, u32[]{:S(2)}) %copy-start) | copy-done | bytes 8388632
  72.8 1.0 copy-done.2
  73.9 1.0 copy-done.4
  74.9 3.6 %finish.1 = (f32[128,2048]{1,0:T(8,128)S(1)}, bf16[128,2048]{1,0:T(8,128)(2,1)S(1)}) custom-call(bf16[16,128,128]{2,1,0:T(8,128)(2,1)S(1)} %bitcast.37, bf16[16,128,128]{2,1,0:T(8,128)(2,1)S(1)} %copy-done.4, f32[16,128,128]{2,1,0:T(8,128)S(1)} %get-tuple-element.12.local_ref, bf16[128,2048]{1,0:T(8,128)(2,1)S(1)} %bitcast.38, f32[1,128]{1,0:T(1,128)S(1)} %bitcast.46, ...), custom_call_target="tpu_custom_call" | custom-call | tf_op jit(solution)/shard_map/finish/pallas_call | solution.py:194
  78.5 2.4 convolution_convert_fusion
  80.9 104.0 %all_to_all.20.x_ref = bf16[128,16,2048]{2,1,0:T(8,128)(2,1)} all-to-all(bf16[128,16,2048]{2,1,0:T(8,128)(2,1)S(1)} %bitcast.49), channel_id=1, replica_groups=mesh['seq'=32,'batch'=4] {'seq','batch'}, dimensions={0} | all-to-all | bytes 16777216 | tf_op jit(solution)/shard_map/all_to_all | solution.py:297
  184.9 20.9 %experts.1 = bf16[128,16,2048]{2,1,0:T(8,128)(2,1)} custom-call(bf16[128,16,2048]{2,1,0:T(8,128)(2,1)} %all_to_all.20.x_ref, bf16[2,2048,1024]{2,1,0:T(8,128)(2,1)} %up_ref.1, bf16[2,512,2048]{2,1,0:T(8,128)(2,1)} %down_ref.1), custom_call_target="tpu_custom_call" | custom-call | tf_op jit(solution)/shard_map/experts/pallas_call | solution.py:234
  205.8 102.4 %all_to_all.21 = bf16[128,16,2048]{2,1,0:T(8,128)(2,1)S(1)} all-to-all(bf16[128,16,2048]{2,1,0:T(8,128)(2,1)} %experts.1), channel_id=1, replica_groups=mesh['seq'=32,'batch'=4] {'seq','batch'}, dimensions={0} | all-to-all | bytes 16777216 | tf_op jit(solution)/shard_map/all_to_all | solution.py:301
  308.2 1.3 fusion.7
  309.5 2.1 fusion.2
  (20 shorter events, 1.2 us)
Async XLA Ops:
  0.0 69.4 %copy-start.1 = (bf16[1,128,2048]{2,1,0:T(8,128)(2,1)S(1)}, bf16[1,128,2048]{2,1,0:T(8,128)(2,1)}, u32[]{:S(2)}) copy-start(bf16[1,128,2048]{2,1,0:T(8,128)(2,1)} %param.17) | copy-start | bytes 1572868
  0.0 1.1 copy-start.5
  1.1 0.9 copy-start.6
  2.1 0.9 copy-start.7
  3.0 0.7 copy-start.8
  3.7 0.7 copy-start.9
  4.4 65.1 %copy-start.10 = (f32[2048]{0:T(1024)S(1)}, f32[2048]{0:T(1024)}, u32[]{:S(2)}) copy-start(f32[2048]{0:T(1024)} %param.23) | copy-start | bytes 24580
  4.4 65.1 %copy-start.11 = (f32[128]{0:T(128)S(1)}, f32[128]{0:T(128)}, u32[]{:S(2)}) copy-start(f32[128]{0:T(128)} %param.20) | copy-start | bytes 1540
  13.4 0.8 copy-start.3
  14.2 32.9 %all-to-all-start = ((bf16[32,208,128]{2,1,0:T(8,128)(2,1)}), bf16[32,208,128]{2,1,0:T(8,128)(2,1)S(1)}, u32[]{:S(2)}, u32[]{:S(2)}) async-start(bf16[32,208,128]{2,1,0:T(8,128)(2,1)} %get-tuple-element.10), calls=%async_computation | async-start | bytes 3407872 | tf_op jit(solution)/shard_map/all_to_all | solution.py:274
  52.1 17.3 %all-to-all-start.1 = ((bf16[32,64,128]{2,1,0:T(8,128)(2,1)}), bf16[32,64,128]{2,1,0:T(8,128)(2,1)S(1)}, u32[]{:S(2)}, u32[]{:S(2)}) async-start(bf16[32,64,128]{2,1,0:T(8,128)(2,1)} %chain.1), calls=%async_computation.1 | async-start | bytes 1048576 | tf_op jit(solution)/shard_map/all_to_all | solution.py:276
  69.5 3.4 %copy-start = (bf16[2048,2048]{1,0:T(8,128)(2,1)S(1)}, bf16[2048,2048]{1,0:T(8,128)(2,1)}, u32[]{:S(2)}) copy-start(bf16[2048,2048]{1,0:T(8,128)(2,1)} %weight_ref.1) | copy-start | bytes 25165828
  72.8 1.0 copy-start.2
  73.9 1.0 copy-start.4

commit v2 on v1

--- a/solution.py
+++ b/solution.py
@@ -11,7 +11,9 @@
 HK = 8
 GROUPS = 2
 ROWS = 8
-MSG = 208
+MSG = 272
+VMEM = 60 << 20
+MESH = pl.DeviceIdType.MESH
 EPSILON = 1e-06
 PRECISE = lax.Precision.HIGHEST
 F32 = jnp.float32
@@ -97,10 +99,9 @@
         line = lax.broadcasted_iota(jnp.int32, (16, DK), 0)
         parts = jnp.where(line == 0, part0.astype(F32), jnp.where(line == 1, part1.astype(F32), part2.astype(F32)))
         parts = jnp.where(line < 3, parts, 0.0).astype(BF16)
-        for half in range(2):
-            msg_ref[2 * h + half, 0:128] = trans
-            msg_ref[2 * h + half, 128:192] = inject[half * 64:(half + 1) * 64]
-            msg_ref[2 * h + half, 192:208] = parts
+        msg_ref[h, 0:128] = trans
+        msg_ref[h, 128:256] = inject
+        msg_ref[h, 256:272] = parts
 
 
 def local_terms(query, key, value, log_decay, strength):
@@ -116,12 +117,12 @@
             pl.BlockSpec((1, heads, TOK), lambda i: (i, 0, 0)),
         ],
         out_specs=[
-            pl.BlockSpec((2 * heads, MSG, DK), lambda i: (i, 0, 0)),
+            pl.BlockSpec((heads, MSG, DK), lambda i: (i, 0, 0)),
             pl.BlockSpec((heads, TOK, DK), lambda i: (i, 0, 0)),
             pl.BlockSpec((heads, TOK, DK), lambda i: (i, 0, 0)),
         ],
         out_shape=[
-            jax.ShapeDtypeStruct((2 * HV, MSG, DK), BF16),
+            jax.ShapeDtypeStruct((HV, MSG, DK), BF16),
             jax.ShapeDtypeStruct((HV, TOK, DK), BF16),
             jax.ShapeDtypeStruct((HV, TOK, DK), F32),
         ],
@@ -130,34 +131,127 @@
             pltpu.VMEM((heads, TOK, TOK), F32),
             pltpu.VMEM((heads, TOK, TOK), BF16),
         ],
-        compiler_params=pltpu.CompilerParams(vmem_limit_bytes=40 << 20),
+        compiler_params=pltpu.CompilerParams(vmem_limit_bytes=VMEM),
         name="local_terms",
     )(query, key, value, log_decay.reshape(GROUPS, heads, TOK), strength.reshape(GROUPS, heads, TOK))
 
 
-def chain_kernel(map_ref, state_ref):
-    count = map_ref.shape[0]
-
-    def step(p, state):
-        high, low = halves(state)
-        state_ref[p] = high
-        both = mul(jnp.concatenate([high, low], axis=0), map_ref[p, 0:128])
-        parts = map_ref[p, 192:208].astype(F32)
-        gamma = parts[0:1] + parts[1:2] + parts[2:3]
-        return state * gamma + (both[:64] + both[64:]) + map_ref[p, 128:192].astype(F32)
-
-    lax.fori_loop(0, count, step, jnp.zeros((64, DK), F32), unroll=4)
-
-
-def chain(maps):
-    count = maps.shape[0]
+PAIRS = (
+    ((1, 1), (3, 3), (1, 3), (3, 1)),
+    ((2, 2),),
+    ((1, 0), (3, 0), (0, 1), (0, 3)),
+    ((2, 0), (0, 2)),
+    ((2, 1), (2, 3)),
+    ((1, 2), (3, 2)),
+)
+
+
+def prefix_kernel(map_ref, state_ref, inbox, outbox, send, receive, send_back, receive_back):
+    seq, batch = lax.axis_index("seq"), lax.axis_index("batch")
+    z, x, core = seq // 8, seq // 2 % 4, seq % 2
+    count = inbox.shape[0]
+    head = z * 4 + x
+
+    barrier = pltpu.get_barrier_semaphore()
+    for other in range(1, count):
+        pl.semaphore_signal(
+            barrier, inc=1, device_id=(lax.rem(seq + other, count), batch), device_id_type=MESH
+        )
+    pl.semaphore_wait(barrier, count - 1)
+
+    def to_owner(p, q):
+        chip = lax.rem(z + p, 4) * 4 + lax.rem(x + q, 4)
+        return pltpu.make_async_remote_copy(
+            map_ref.at[chip], inbox.at[seq], send.at[p * 4 + q], receive.at[seq],
+            device_id=(chip * 2, batch), device_id_type=MESH,
+        )
+
+    def own():
+        return pltpu.make_async_copy(map_ref.at[head], inbox.at[seq], receive.at[seq])
+
+    def back(place):
+        return pltpu.make_async_remote_copy(
+            outbox.at[place], state_ref.at[head], send_back.at[place], receive_back.at[head],
+            device_id=(place, batch), device_id_type=MESH,
+        )
+
+    def own_back():
+        return pltpu.make_async_copy(outbox.at[seq], state_ref.at[head], receive_back.at[head])
+
+    far = [offset for group in PAIRS for offset in group]
+    for p, q in far:
+        to_owner(p, q).start()
+
+    @pl.when(core == 1)
+    def _():
+        to_owner(0, 0).start()
+
+    @pl.when(core == 0)
+    def _():
+        own().start()
+
+        def step(place, state):
+            pltpu.make_async_copy(inbox.at[place], inbox.at[place], receive.at[place]).wait()
+            high, low = halves(state)
+            outbox[place] = high
+
+            @pl.when(place == seq)
+            def _():
+                own_back().start()
+
+            @pl.when(place != seq)
+            def _():
+                back(place).start()
+
+            both = mul(jnp.concatenate([high, low], axis=0), inbox[place, 0:128])
+            parts = inbox[place, 256:272].astype(F32)
+            gamma = parts[0:1] + parts[1:2] + parts[2:3]
+            return state * gamma + (both[:DK] + both[DK:]) + inbox[place, 128:256].astype(F32)
+
+        lax.fori_loop(0, count, step, jnp.zeros((DK, DK), F32))
+
+        def sent(place, carry):
+            @pl.when(place != seq)
+            def _():
+                back(place).wait_send()
+
+            return carry
+
+        lax.fori_loop(0, count, sent, 0)
+
+    for p, q in far:
+        to_owner(p, q).wait_send()
+
+    @pl.when(core == 1)
+    def _():
+        to_owner(0, 0).wait_send()
+
+    def arrived(place, carry):
+        pltpu.make_async_copy(state_ref.at[place], state_ref.at[place], receive_back.at[place]).wait()
+        return carry
+
+    lax.fori_loop(0, HV, arrived, 0)
+
+
+def prefix(maps, count):
+    dma = pltpu.SemaphoreType.DMA
     return pl.pallas_call(
-        chain_kernel,
-        out_shape=jax.ShapeDtypeStruct((count, 64, DK), BF16),
+        prefix_kernel,
+        out_shape=jax.ShapeDtypeStruct((HV, DK, DK), BF16),
         in_specs=[pl.BlockSpec(memory_space=pltpu.VMEM)],
         out_specs=pl.BlockSpec(memory_space=pltpu.VMEM),
-        compiler_params=pltpu.CompilerParams(vmem_limit_bytes=40 << 20),
-        name="chain",
+        scratch_shapes=[
+            pltpu.VMEM((count, MSG, DK), BF16),
+            pltpu.VMEM((count, DK, DK), BF16),
+            dma((HV,)),
+            dma((count,)),
+            dma((count,)),
+            dma((HV,)),
+        ],
+        compiler_params=pltpu.CompilerParams(
+            collective_id=0, has_side_effects=True, vmem_limit_bytes=VMEM
+        ),
+        name="prefix",
     )(maps)
 
 
@@ -207,7 +301,7 @@
         out_specs=[pl.BlockSpec((TOK, width), whole2), pl.BlockSpec((TOK, width), whole2)],
         out_shape=[jax.ShapeDtypeStruct((TOK, width), F32), jax.ShapeDtypeStruct((TOK, width), BF16)],
         scratch_shapes=[pltpu.VMEM((TOK, HV * DK), BF16)],
-        compiler_params=pltpu.CompilerParams(vmem_limit_bytes=40 << 20),
+        compiler_params=pltpu.CompilerParams(vmem_limit_bytes=VMEM),
         name="finish",
     )(state, reader, local, gate, gain[None], weight, resid, post[None])
 
@@ -241,7 +335,7 @@
         ],
         out_specs=pl.BlockSpec((tile, rows, width), lambda i: (i, 0, 0)),
         out_shape=jax.ShapeDtypeStruct(x.shape, BF16),
-        compiler_params=pltpu.CompilerParams(vmem_limit_bytes=56 << 20),
+        compiler_params=pltpu.CompilerParams(vmem_limit_bytes=VMEM),
         name="experts",
     )(x, up, down)
 
@@ -271,11 +365,9 @@
     maps, reader, local = local_terms(
         query_rows[0], key_rows[0], value_rows[0], log_decay[0], write_strength[0]
     )
-    maps = lax.all_to_all(maps, "seq", split_axis=0, concat_axis=0, tiled=True)
-    states = chain(maps)
-    states = lax.all_to_all(states, "seq", split_axis=0, concat_axis=0, tiled=True)
+    states = prefix(maps, lax.axis_size("seq"))
     mid, moe_in = finish(
-        states.reshape(HV, DK, DK), reader, local, gate_z[0], norm_gain, out_weight, residual[0], post_gain
+        states, reader, local, gate_z[0], norm_gain, out_weight, residual[0], post_gain
     )
 
     ids = expert_ids[0]

time: 312 us -> 293 us (0.939)
  waiting for transfers between devices: 32.5 us -> 0 us
  Pallas kernels: 38.4 us -> 70.3 us
  starting transfers between devices: 15.1 us -> 0 us
  local copies, waits for them, and re-layouts: 11.5 us -> 0.82 us
  blocking collectives: 206 us -> 213 us
    all_to_all x2 -> x0, waiting for transfers between devices: 32.5 us -> none  [the longest x1 22 us: shards(): maps = lax.all_to_all(maps, 'seq', split_axis=0, concat_axis=0, tiled=True)]
    pallas_call x1, Pallas kernels: 4.93 us -> 31.2 us  [prefix(): pl.pallas_call(prefix_kernel, out_shape=jax.ShapeDtypeStruct((HV, DK, DK)...]
    all_to_all x2 -> x0, starting transfers between devices: 15.1 us -> none  [the longest x1 9.43 us: shards(): maps = lax.all_to_all(maps, 'seq', split_axis=0, concat_axis=0, tiled=True)]
    unnamed x25 -> x3, local copies, waits for them, and re-layouts: 11.4 us -> 0.7 us
    all_to_all x1, blocking collectives: 104 us -> 111 us  [shards(): lax.all_to_all(outgoing.reshape(devices, exp_dev * ROWS, width), ('seq',...]
    pallas_call x1, Pallas kernels: 3.55 us -> 8.02 us  [finish(): pl.pallas_call(finish_kernel, grid=(width // tile,), in_specs=[pl.BlockSp...]
  transfers between devices with their start and end apart: 2 -> 0, of which waited for: 2 -> 0; matrix products, arithmetic and copies ran while one was open for 1% -> 0% of each run, Pallas kernels for 0% -> 0%
where the time goes in v2:
time: 293 us
  blocking collectives  213 us (73%)
  Pallas kernels  70.3 us (24%)
  matrix products  6.93 us (2%)
    all_to_all x1, blocking collectives, shards(): lax.all_to_all(outgoing.reshape(devices, exp_dev * ROWS, width), ('seq',...  111 us
    all_to_all x1, blocking collectives, shards(): lax.all_to_all(result, ('seq', 'batch'), split_axis=0, concat_axis=0, til...  102 us
    pallas_call x1, Pallas kernels, prefix(): pl.pallas_call(prefix_kernel, out_shape=jax.ShapeDtypeStruct((HV, DK, DK)...  31.2 us
    pallas_call x1, Pallas kernels, experts(): pl.pallas_call(expert_kernel, grid=(count // tile,), in_specs=[pl.BlockSp...  20.9 us
    pallas_call x1, Pallas kernels, local_terms(): pl.pallas_call(local_kernel, grid=(GROUPS,), in_specs=[pl.BlockSpec((TOK,...  10.2 us
    pallas_call x1, Pallas kernels, finish(): pl.pallas_call(finish_kernel, grid=(width // tile,), in_specs=[pl.BlockSp...  8.02 us

profile of v2, /device:TPU:1, one launch (start us, length us, event | category | flops | bytes accessed | tf_op | source)
XLA Modules:
  0.0 292.9 jit_solution(11492198743740140380)
XLA Ops:
  0.0 0.7 reduce_sum.28
  0.7 0.7 fusion.22
  1.4 0.7 copy.19
  2.1 0.1 eq.60
  2.2 0.2 select_reduce_fusion
  2.5 0.1 convolution_select_fusion
  2.6 10.2 %local_terms.1 = (bf16[16,272,128]{2,1,0:T(8,128)(2,1)}, bf16[16,128,128]{2,1,0:T(8,128)(2,1)}, f32[16,128,128]{2,1,0:T(8,128)}) custom-call(bf16[128,1024]{1,0:T(8,128)(2,1)} %bitcast.42, bf16[128,1024]{1,0:T(8,128)(2,1)} %bitcast.43, bf16[128,2048]{1,0:T(8,128)(2,1)} %bitcast.41, f32[2,8,128]{2,1,0:T(8,128)} %bitcast.45, f32[2,8,128]{2,1,0:T(8,128)} %bitcast.46), custom_call_target="tpu_custom_call" | custom-call | tf_op jit(solution)/shard_map/local_terms/pallas_call | solution.py:109
  12.8 31.2 %prefix.1.state_ref = bf16[16,128,128]{2,1,0:T(8,128)(2,1)} custom-call(bf16[16,272,128]{2,1,0:T(8,128)(2,1)} %get-tuple-element.10.map_ref), custom_call_target="tpu_custom_call" | custom-call | tf_op jit(solution)/shard_map/prefix/pallas_call | solution.py:238
  44.0 8.0 %finish.1 = (f32[128,2048]{1,0:T(8,128)}, bf16[128,2048]{1,0:T(8,128)(2,1)}) custom-call(bf16[16,128,128]{2,1,0:T(8,128)(2,1)} %prefix.1.state_ref, bf16[16,128,128]{2,1,0:T(8,128)(2,1)} %get-tuple-element.11.reader_ref, f32[16,128,128]{2,1,0:T(8,128)} %get-tuple-element.12.local_ref, bf16[128,2048]{1,0:T(8,128)(2,1)} %bitcast.39, f32[1,128]{1,0:T(1,128)} %bitcast.48, ...), custom_call_target="tpu_custom_call" | custom-call | tf_op jit(solution)/shard_map/finish/pallas_call | solution.py:288
  52.0 3.4 %convolution_convert_fusion = bf16[2048,2048]{1,0:T(8,128)(2,1)S(1)} fusion(bf16[128,2048]{1,0:T(8,128)(2,1)} %get-tuple-element.14, f32[2048]{0:T(1024)S(1)} %eq.60, f32[256,128]{1,0:T(8,128)S(1)} %convolution_select_fusion), kind=kOutput, calls=%fused_computation | convolution fusion | flops 1078198272 | bytes 9052160 | tf_op jit(solution)/shard_map/dot_general | solution.py:388
  55.4 110.7 %all_to_all.10.x_ref = bf16[128,16,2048]{2,1,0:T(8,128)(2,1)} all-to-all(bf16[128,16,2048]{2,1,0:T(8,128)(2,1)S(1)} %bitcast.38), channel_id=1, replica_groups=mesh['seq'=32,'batch'=4] {'seq','batch'}, dimensions={0} | all-to-all | bytes 16777216 | tf_op jit(solution)/shard_map/all_to_all | solution.py:389
  166.1 20.9 %experts.1 = bf16[128,16,2048]{2,1,0:T(8,128)(2,1)} custom-call(bf16[128,16,2048]{2,1,0:T(8,128)(2,1)} %all_to_all.10.x_ref, bf16[2,2048,1024]{2,1,0:T(8,128)(2,1)} %up_ref.1, bf16[2,512,2048]{2,1,0:T(8,128)(2,1)} %down_ref.1), custom_call_target="tpu_custom_call" | custom-call | tf_op jit(solution)/shard_map/experts/pallas_call | solution.py:328
  187.1 102.4 %all_to_all.11 = bf16[128,16,2048]{2,1,0:T(8,128)(2,1)S(1)} all-to-all(bf16[128,16,2048]{2,1,0:T(8,128)(2,1)} %experts.1), channel_id=1, replica_groups=mesh['seq'=32,'batch'=4] {'seq','batch'}, dimensions={0} | all-to-all | bytes 16777216 | tf_op jit(solution)/shard_map/all_to_all | solution.py:393
  289.5 0.0 copy-start
  289.5 1.3 fusion.7
  290.8 0.0 copy-done
  290.8 2.1 fusion.2
  (1 shorter events, 0.0 us)
Async XLA Ops:
  289.5 1.3 copy-start

commit v3 on v2

--- a/solution.py
+++ b/solution.py
@@ -1,3 +1,5 @@
+import functools
+
 import jax
 import jax.numpy as jnp
 from jax import lax
@@ -13,6 +15,7 @@
 ROWS = 8
 MSG = 272
 VMEM = 60 << 20
+PARTS = ((0, 768), (768, 1408), (1408, 2048))
 MESH = pl.DeviceIdType.MESH
 EPSILON = 1e-06
 PRECISE = lax.Precision.HIGHEST
@@ -136,6 +139,46 @@
     )(query, key, value, log_decay.reshape(GROUPS, heads, TOK), strength.reshape(GROUPS, heads, TOK))
 
 
+def axis_names():
+    seq = lax.axis_index("seq")
+    return (lax.div(seq, 8), lax.rem(lax.div(seq, 2), 4), lax.rem(seq, 2), lax.axis_index("batch"))
+
+
+def device_at(offset):
+    z, x, core, y = axis_names()
+    dz, dx, dcore, dy = offset
+    seq = lax.rem(z + dz, 4) * 8 + lax.rem(x + dx, 4) * 2 + lax.rem(core + dcore, 2)
+    return (seq, lax.rem(y + dy, 4))
+
+
+def greet(offsets):
+    barrier = pltpu.get_barrier_semaphore()
+    for offset in offsets:
+        pl.semaphore_signal(barrier, inc=1, device_id=device_at(offset), device_id_type=MESH)
+    pl.semaphore_wait(barrier, len(offsets))
+
+
+def along(part, d):
+    return ((0, 0, 0, d), (0, d, 0, 0), (d, 0, 0, 0))[part]
+
+
+def across(part, p, q, dcore):
+    return ((p, q, dcore, 0), (p, 0, dcore, q), (0, p, dcore, q))[part]
+
+
+def line_place(part):
+    z, x, _, y = axis_names()
+    return (y, x, z)[part]
+
+
+def plane_index(part, offset):
+    z, x, core, y = axis_names()
+    dz, dx, dcore, dy = offset
+    z, x, y = lax.rem(z + dz, 4), lax.rem(x + dx, 4), lax.rem(y + dy, 4)
+    first, second = ((z, x), (z, y), (x, y))[part]
+    return (first * 4 + second) * 2 + lax.rem(core + dcore, 2)
+
+
 PAIRS = (
     ((1, 1), (3, 3), (1, 3), (3, 1)),
     ((2, 2),),
@@ -146,7 +189,25 @@
 )
 
 
-def prefix_kernel(map_ref, state_ref, inbox, outbox, send, receive, send_back, receive_back):
+def line_copies(sources, targets, semaphores, scatter):
+    send, receive, own = semaphores
+    copies = []
+    for part in range(3):
+        place = line_place(part)
+        source = sources[part].at[place] if scatter else sources[part]
+        copies.append(pltpu.make_async_copy(source, targets[part].at[place], own.at[part]))
+    for d in (1, 3, 2):
+        for part in range(3):
+            place = line_place(part)
+            source = sources[part].at[lax.rem(place + d, 4)] if scatter else sources[part]
+            copies.append(pltpu.make_async_remote_copy(
+                source, targets[part].at[place], send.at[part, d], receive.at[part, d],
+                device_id=device_at(along(part, d)), device_id_type=MESH,
+            ))
+    return copies
+
+
+def prefix_kernel(map_ref, table_ref, state_ref, tables_ref, inbox, outbox, send, receive, send_back, receive_back, *lines):
     seq, batch = lax.axis_index("seq"), lax.axis_index("batch")
     z, x, core = seq // 8, seq // 2 % 4, seq % 2
     count = inbox.shape[0]
@@ -157,7 +218,12 @@
         pl.semaphore_signal(
             barrier, inc=1, device_id=(lax.rem(seq + other, count), batch), device_id_type=MESH
         )
-    pl.semaphore_wait(barrier, count - 1)
+    for d in (1, 2, 3):
+        pl.semaphore_signal(barrier, inc=1, device_id=device_at((0, 0, 0, d)), device_id_type=MESH)
+    pl.semaphore_wait(barrier, count + 2)
+    tables = line_copies((table_ref,) * 3, [tables_ref.at[part] for part in range(3)], lines, False)
+    for copy in tables:
+        copy.start()
 
     def to_owner(p, q):
         chip = lax.rem(z + p, 4) * 4 + lax.rem(x + q, 4)
@@ -231,15 +297,20 @@
         return carry
 
     lax.fori_loop(0, HV, arrived, 0)
-
-
-def prefix(maps, count):
+    for copy in tables:
+        copy.wait()
+
+
+def prefix(maps, table, count):
     dma = pltpu.SemaphoreType.DMA
     return pl.pallas_call(
         prefix_kernel,
-        out_shape=jax.ShapeDtypeStruct((HV, DK, DK), BF16),
-        in_specs=[pl.BlockSpec(memory_space=pltpu.VMEM)],
-        out_specs=pl.BlockSpec(memory_space=pltpu.VMEM),
+        out_shape=[
+            jax.ShapeDtypeStruct((HV, DK, DK), BF16),
+            jax.ShapeDtypeStruct((3, 4) + table.shape, BF16),
+        ],
+        in_specs=[pl.BlockSpec(memory_space=pltpu.VMEM)] * 2,
+        out_specs=[pl.BlockSpec(memory_space=pltpu.VMEM)] * 2,
         scratch_shapes=[
             pltpu.VMEM((count, MSG, DK), BF16),
             pltpu.VMEM((count, DK, DK), BF16),
@@ -247,15 +318,18 @@
             dma((count,)),
             dma((count,)),
             dma((HV,)),
+            dma((3, 4)),
+            dma((3, 4)),
+            dma((3,)),
         ],
         compiler_params=pltpu.CompilerParams(
             collective_id=0, has_side_effects=True, vmem_limit_bytes=VMEM
         ),
         name="prefix",
-    )(maps)
-
-
-def finish_kernel(state_ref, reader_ref, local_ref, gate_ref, gain_ref, weight_ref, resid_ref, post_ref, mid_ref, moe_ref, normed_ref):
+    )(maps, table)
+
+
+def finish_kernel(state_ref, reader_ref, local_ref, gate_ref, gain_ref, weight_ref, resid_ref, post_ref, mid_ref, a_ref, b_ref, c_ref, normed_ref):
     step = pl.program_id(0)
     width = weight_ref.shape[1]
 
@@ -275,9 +349,11 @@
     @pl.when(step == pl.num_programs(0) - 1)
     def _():
         mid = mid_ref[...]
-        moe_ref[...] = (
+        moe_in = (
             mid * lax.rsqrt(jnp.mean(mid * mid, axis=-1, keepdims=True) + EPSILON) * post_ref[...]
         ).astype(BF16)
+        for ref, (low, high) in zip((a_ref, b_ref, c_ref), PARTS):
+            ref[...] = moe_in[:, low:high]
 
 
 def finish(state, reader, local, gate, gain, weight, resid, post):
@@ -298,46 +374,249 @@
             pl.BlockSpec((TOK, width), whole2),
             pl.BlockSpec((1, width), whole2),
         ],
-        out_specs=[pl.BlockSpec((TOK, width), whole2), pl.BlockSpec((TOK, width), whole2)],
-        out_shape=[jax.ShapeDtypeStruct((TOK, width), F32), jax.ShapeDtypeStruct((TOK, width), BF16)],
+        out_specs=[pl.BlockSpec((TOK, width), whole2)]
+        + [pl.BlockSpec((TOK, high - low), whole2) for low, high in PARTS],
+        out_shape=[jax.ShapeDtypeStruct((TOK, width), F32)]
+        + [jax.ShapeDtypeStruct((TOK, high - low), BF16) for low, high in PARTS],
         scratch_shapes=[pltpu.VMEM((TOK, HV * DK), BF16)],
         compiler_params=pltpu.CompilerParams(vmem_limit_bytes=VMEM),
         name="finish",
     )(state, reader, local, gate, gain[None], weight, resid, post[None])
 
 
-def expert_kernel(x_ref, up_ref, down_ref, y_ref):
-    sources, _, width = x_ref.shape
+ORDER = [(p, q, dcore) for group in PAIRS for dcore in (0, 1) for p, q in group] + [(0, 0, 1), (0, 0, 0)]
+
+
+def plane_copy(source, target, send, receive, part, step):
+    p, q, dcore = step
+    offset = across(part, p, q, dcore)
+    slot = p * 8 + q * 2 + dcore
+    if step == (0, 0, 0):
+        return pltpu.make_async_copy(source, target, receive.at[part, slot])
+    return pltpu.make_async_remote_copy(
+        source, target, send.at[part, slot], receive.at[part, slot],
+        device_id=device_at(offset), device_id_type=MESH,
+    )
+
+
+def wait_sent(copy, step):
+    if step != (0, 0, 0):
+        copy.wait_send()
+
+
+def wait_arrived(copy, step):
+    if step == (0, 0, 0):
+        copy.wait()
+    else:
+        copy.wait_recv()
+
+
+def plane_offsets():
+    return sorted(set(across(part, *step) for part in range(3) for step in ORDER) - {(0, 0, 0, 0)})
+
+
+def picked(slot):
+    rows = lax.broadcasted_iota(jnp.int32, (ROWS, TOK), 0).astype(F32)
+    return slot[..., None, :] == rows
+
+
+def dispatch_kernel(*refs):
+    slot_ref, rows, outs = refs[0], refs[1:4], refs[4:7]
+    lines, stages = refs[7:10], refs[10:13]
+    line_semaphores, (send, receive) = refs[13:16], refs[16:18]
+    greet(plane_offsets())
+    gathers = line_copies(rows, lines, line_semaphores, False)
+    for copy in gathers:
+        copy.start()
+    for copy in gathers:
+        copy.wait()
+    copies = []
+    for g in range(4):
+        steps = ORDER[8 * g:8 * g + 8]
+        for part in range(3):
+            places = [plane_index(part, across(part, *step)) for step in steps]
+
+            def fill(a, carry, part=part, places=places, g=g):
+                slots = jnp.concatenate([slot_ref[part, place, a] for place in places], axis=0)
+                take = jnp.where(picked(slots), 1.0, 0.0).reshape(16 * ROWS, TOK).astype(BF16)
+                packed = mul(take, lines[part][a]).astype(BF16)
+                stages[part][8 * g:8 * g + 8, a] = packed.reshape(8, 2 * ROWS, packed.shape[1])
+                return carry
+
+            lax.fori_loop(0, 4, fill, 0)
+            here = plane_index(part, (0, 0, 0, 0))
+            for i, step in enumerate(steps):
+                copy = plane_copy(stages[part].at[8 * g + i], outs[part].at[here], send, receive, part, step)
+                copy.start()
+                copies.append((copy, step))
+    for copy, step in copies:
+        wait_sent(copy, step)
+        wait_arrived(copy, step)
+
+
+def dispatch(slots, rows):
+    dma = pltpu.SemaphoreType.DMA
+    shapes = [(32, 4, 2 * ROWS, part.shape[1]) for part in rows]
+    return pl.pallas_call(
+        dispatch_kernel,
+        in_specs=[pl.BlockSpec(memory_space=pltpu.VMEM)] * 4,
+        out_specs=[pl.BlockSpec(memory_space=pl.ANY)] * 3,
+        out_shape=[jax.ShapeDtypeStruct(shape, BF16) for shape in shapes],
+        scratch_shapes=[pltpu.VMEM((4,) + part.shape, BF16) for part in rows]
+        + [pltpu.VMEM(shape, BF16) for shape in shapes]
+        + [dma((3, 4)), dma((3, 4)), dma((3,)), dma((3, 32)), dma((3, 32))],
+        compiler_params=pltpu.CompilerParams(
+            collective_id=1, has_side_effects=True, vmem_limit_bytes=VMEM
+        ),
+        name="dispatch",
+    )(slots, *rows)
+
+
+def collect_kernel(*refs):
+    slot_ref, share_ref, mid_ref, results, out_ref = refs[0], refs[1], refs[2], refs[3:6], refs[6]
+    landed, partials, sums = refs[7:10], refs[10:13], refs[13:16]
+    send, receive = refs[16:18]
+    line_semaphores = refs[18:21]
+    greet(plane_offsets())
+    copies = [[], [], []]
+    for step in ORDER:
+        for part in range(3):
+            target = landed[part].at[plane_index(part, (0, 0, 0, 0))]
+            source = results[part].at[plane_index(part, across(part, *step))]
+            copy = plane_copy(source, target, send, receive, part, step)
+            copy.start()
+            copies[part].append((copy, step))
+    lines = line_copies(partials, sums, line_semaphores, True)
+    own, others = lines[0:3], lines[3:]
+    for part in range(3):
+        for copy, step in copies[part]:
+            wait_arrived(copy, step)
+        width = landed[part].shape[3]
+        for n, d in enumerate((1, 3, 2, 0)):
+            a = lax.rem(line_place(part) + d, 4)
+            slot = slot_ref[part, :, a]
+            give = jnp.where(picked(slot), share_ref[part, :, a][:, :, None, :], 0.0)
+            high, low = halves(give.reshape(64 * ROWS, TOK))
+            rows = landed[part][:, a].reshape(64 * ROWS, width)
+            both = mul(jnp.concatenate([high, low], axis=1), rows, TN)
+            partials[part][a] = (both[:TOK] + both[TOK:]).astype(BF16)
+            copy = own[part] if d == 0 else others[3 * n + part]
+            copy.start()
+    for part, (low, high) in enumerate(PARTS):
+        for n in range(3):
+            others[3 * n + part].wait()
+        own[part].wait()
+        total = mid_ref[:, low:high]
+        for a in range(4):
+            total = total + sums[part][a].astype(F32)
+        out_ref[:, low:high] = total.astype(BF16)
+    for part in range(3):
+        for copy, step in copies[part]:
+            wait_sent(copy, step)
+
+
+def collect(slots, shares, mid, results):
+    dma = pltpu.SemaphoreType.DMA
+    widths = [part.shape[3] for part in results]
+    return pl.pallas_call(
+        collect_kernel,
+        in_specs=[pl.BlockSpec(memory_space=pltpu.VMEM)] * 3 + [pl.BlockSpec(memory_space=pl.ANY)] * 3,
+        out_specs=pl.BlockSpec(memory_space=pltpu.VMEM),
+        out_shape=jax.ShapeDtypeStruct(mid.shape, BF16),
+        scratch_shapes=[pltpu.VMEM(part.shape, BF16) for part in results]
+        + [pltpu.VMEM((4, TOK, width), BF16) for width in widths] * 2
+        + [dma((3, 32)), dma((3, 32)), dma((3, 4)), dma((3, 4)), dma((3,))],
+        compiler_params=pltpu.CompilerParams(
+            collective_id=2, has_side_effects=True, vmem_limit_bytes=VMEM
+        ),
+        name="collect",
+    )(slots, shares, mid, *results)
+
+
+def part_views(parts):
+    a, b, c = parts
+    return (
+        a.reshape(4, 4, 2, 4, 2 * ROWS, a.shape[3]),
+        b.reshape(4, 4, 2, 4, 2 * ROWS, b.shape[3]),
+        c.reshape(4, 4, 2, 4, 2 * ROWS, c.shape[3]),
+    )
+
+
+def expert_kernel(a_ref, b_ref, c_ref, up_ref, down_ref, ya_ref, yb_ref, yc_ref, x_ref, y_ref):
     hidden_width = down_ref.shape[1]
-    rows = sources * ROWS
-    x = x_ref[...].astype(F32)
+    wa, wb = a_ref.shape[5], b_ref.shape[5]
+    width = x_ref.shape[2]
+    sources = [(x * 8 + core * 4 + y, x, core, y) for x in range(4) for core in range(2) for y in range(4)]
+    for n, x, core, y in sources:
+        x_ref[n, :, 0:wa] = a_ref[0, x, core, y]
+        x_ref[n, :, wa:wa + wb] = b_ref[0, y, core, x]
+        x_ref[n, :, wa + wb:] = c_ref[x, y, core, 0]
+    rows = len(sources) * ROWS
+    x_all = x_ref[...].astype(F32)
     results = []
     for j in range(2):
-        mine = x[:, j * ROWS:(j + 1) * ROWS].reshape(rows, width).astype(BF16)
+        mine = x_all[:, j * ROWS:(j + 1) * ROWS].reshape(rows, width).astype(BF16)
         gate = mul(mine, up_ref[j, :, :hidden_width])
         lift = mul(mine, up_ref[j, :, hidden_width:])
         hidden = (gate / (1.0 + jnp.exp(-gate)) * lift).astype(BF16)
-        results.append(mul(hidden, down_ref[j]).reshape(sources, ROWS, width))
+        results.append(mul(hidden, down_ref[j]).reshape(len(sources), ROWS, width))
     y_ref[...] = jnp.concatenate(results, axis=1).astype(BF16)
-
-
-def experts(x, up, down):
-    count, rows, width = x.shape
-    tile = 32
-    whole3 = lambda i: (0, 0, 0)
-    return pl.pallas_call(
+    for n, x, core, y in sources:
+        ya_ref[0, x, core, y] = y_ref[n, :, 0:wa]
+        yb_ref[0, y, core, x] = y_ref[n, :, wa:wa + wb]
+        yc_ref[x, y, core, 0] = y_ref[n, :, wa + wb:]
+
+
+def experts(parts, up, down):
+    views = part_views(parts)
+    width = up.shape[1]
+    whole3 = lambda z: (0, 0, 0)
+    first = lambda z: (z, 0, 0, 0, 0, 0)
+    last = lambda z: (0, 0, 0, z, 0, 0)
+    specs = [
+        pl.BlockSpec((1,) + views[0].shape[1:], first),
+        pl.BlockSpec((1,) + views[1].shape[1:], first),
+        pl.BlockSpec(views[2].shape[:3] + (1,) + views[2].shape[4:], last),
+    ]
+    results = pl.pallas_call(
         expert_kernel,
-        grid=(count // tile,),
-        in_specs=[
-            pl.BlockSpec((tile, rows, width), lambda i: (i, 0, 0)),
+        grid=(4,),
+        in_specs=specs + [
             pl.BlockSpec(up.shape, whole3, pipeline_mode=pl.Buffered(1)),
             pl.BlockSpec(down.shape, whole3, pipeline_mode=pl.Buffered(1)),
         ],
-        out_specs=pl.BlockSpec((tile, rows, width), lambda i: (i, 0, 0)),
-        out_shape=jax.ShapeDtypeStruct(x.shape, BF16),
+        out_specs=specs,
+        out_shape=[jax.ShapeDtypeStruct(view.shape, BF16) for view in views],
+        scratch_shapes=[pltpu.VMEM((32, 2 * ROWS, width), BF16), pltpu.VMEM((32, 2 * ROWS, width), BF16)],
         compiler_params=pltpu.CompilerParams(vmem_limit_bytes=VMEM),
         name="experts",
-    )(x, up, down)
+    )(*views, up, down)
+    return [result.reshape(part.shape) for result, part in zip(results, parts)]
+
+
+def routing_table(ids, weights):
+    high, low = halves(weights)
+    return jnp.concatenate([ids.T.astype(BF16), high.T, low.T, jnp.zeros((2, TOK), BF16)], axis=0)
+
+
+def routes(tables, top, exp_dev):
+    z, x, core, y = axis_names()
+    place = jnp.arange(32, dtype=jnp.int32)
+    first, second, side = place // 8, place // 2 % 4, place % 2
+    device = jnp.stack([
+        place * 4 + y,
+        (first * 8 + x * 2 + side) * 4 + second,
+        (z * 8 + first * 2 + side) * 4 + second,
+    ])
+    numbers = tables[:, :, 0:top].astype(F32)
+    share = tables[:, :, top:2 * top].astype(F32) + tables[:, :, 2 * top:3 * top].astype(F32)
+    expert = (device[:, :, None] * exp_dev + jnp.arange(exp_dev)).astype(F32)
+    named = numbers[:, None, :, None] == expert[:, :, None, :, None, None]
+    chosen = jnp.sum(named.astype(F32), axis=4)
+    given = jnp.sum(jnp.where(named, share[:, None, :, None], 0.0), axis=4)
+    earlier = jnp.triu(jnp.ones((TOK, TOK), BF16), 1)
+    rank = mul(chosen.astype(BF16).reshape(-1, TOK), earlier).reshape(chosen.shape)
+    return jnp.where(chosen > 0, rank, -1.0), given
 
 
 def shards(
@@ -356,44 +635,21 @@
     expert_up,
     expert_down,
 ):
-    width = residual.shape[2]
-    devices = lax.axis_size("seq") * lax.axis_size("batch")
     exp_dev = expert_up.shape[0]
-    total_experts = exp_dev * devices
-    slots = total_experts * ROWS
-
+    scores = gate_scores[0]
+    weights = scores / jnp.sum(scores, axis=-1, keepdims=True)
+    table = routing_table(expert_ids[0], weights)
     maps, reader, local = local_terms(
         query_rows[0], key_rows[0], value_rows[0], log_decay[0], write_strength[0]
     )
-    states = prefix(maps, lax.axis_size("seq"))
-    mid, moe_in = finish(
+    states, tables = prefix(maps, table, lax.axis_size("seq"))
+    mid, *rows = finish(
         states, reader, local, gate_z[0], norm_gain, out_weight, residual[0], post_gain
     )
-
-    ids = expert_ids[0]
-    scores = gate_scores[0]
-    weights = scores / jnp.sum(scores, axis=-1, keepdims=True)
-    named = ids.T[:, None, :] == jnp.arange(total_experts, dtype=jnp.int32)[None, :, None]
-    chosen = jnp.sum(named.astype(F32), axis=0)
-    share = jnp.sum(jnp.where(named, weights.T[:, None, :], 0.0), axis=0)
-    earlier = jnp.triu(jnp.ones((TOK, TOK), BF16), 1)
-    rank = jnp.dot(chosen.astype(BF16), earlier, preferred_element_type=F32)
-    place = jnp.where(chosen > 0, rank, -1.0)
-    pick = place[:, None, :] == jnp.arange(ROWS, dtype=F32)[None, :, None]
-    take = pick.astype(BF16).reshape(slots, TOK)
-    give = jnp.where(pick, share[:, None, :], 0.0).reshape(slots, TOK)
-    give_high = give.astype(BF16)
-    give_low = (give - give_high.astype(F32)).astype(BF16)
-
-    outgoing = jnp.dot(take, moe_in, preferred_element_type=F32).astype(BF16)
-    arrived = lax.all_to_all(
-        outgoing.reshape(devices, exp_dev * ROWS, width), ("seq", "batch"), split_axis=0, concat_axis=0, tiled=True
-    )
-    result = experts(arrived, expert_up, expert_down)
-    returned = lax.all_to_all(result, ("seq", "batch"), split_axis=0, concat_axis=0, tiled=True)
-    returned = returned.reshape(slots, width)
-    mixed = mid + (mul(give_high, returned, TN) + mul(give_low, returned, TN))
-    return mixed.astype(BF16)[None]
+    slots, shares = routes(tables, expert_ids.shape[2], exp_dev)
+    arrived = dispatch(slots, rows)
+    results = experts(arrived, expert_up, expert_down)
+    return collect(slots, shares, mid, results)[None]
 
 
 def solution(mesh):

time: 293 us -> 271 us (0.925)
  blocking collectives: 213 us -> 0 us
  Pallas kernels: 70.3 us -> 262 us
  matrix products: 6.93 us -> 0.18 us
  other arithmetic: 1.65 us -> 5.05 us
    all_to_all x2 -> x0, blocking collectives: 213 us -> none  [the longest x1 111 us: shards(): lax.all_to_all(outgoing.reshape(devices, exp_dev * ROWS, width), ('seq',...]
    pallas_call x2 -> x4, Pallas kernels: 52.1 us -> 244 us  [the longest x1 95.9 us: collect(): pl.pallas_call(collect_kernel, in_specs=[pl.BlockSpec(memory_space=pltpu....]
    dot_general x2 -> x0, matrix products: 3.56 us -> none  [the longest x1 3.41 us: shards(): outgoing = jnp.dot(take, moe_in, preferred_element_type=F32).astype(BF16)]
    dot_general x2 -> x1, matrix products: 3.38 us -> 0.18 us  [mul(): return lax.dot_general(a, b, dims, preferred_element_type=F32)]
where the time goes in v3:
time: 271 us
  Pallas kernels  262 us (97%)
  other arithmetic  5.05 us (2%)
  local copies, waits for them, and re-layouts  3.03 us (1%)
    pallas_call x1, Pallas kernels, collect(): pl.pallas_call(collect_kernel, in_specs=[pl.BlockSpec(memory_space=pltpu....  95.9 us
    pallas_call x1, Pallas kernels, dispatch(): pl.pallas_call(dispatch_kernel, in_specs=[pl.BlockSpec(memory_space=pltpu...  95.5 us
    pallas_call x1, Pallas kernels, prefix(): pl.pallas_call(prefix_kernel, out_shape=[jax.ShapeDtypeStruct((HV, DK, DK...  31.8 us
    pallas_call x1, Pallas kernels, experts(): pl.pallas_call(expert_kernel, grid=(4,), in_specs=specs + [pl.BlockSpec(u...  21.2 us
    pallas_call x1, Pallas kernels, local_terms(): pl.pallas_call(local_kernel, grid=(GROUPS,), in_specs=[pl.BlockSpec((TOK,...  10.2 us
    pallas_call x1, Pallas kernels, finish(): pl.pallas_call(finish_kernel, grid=(width // tile,), in_specs=[pl.BlockSp...  8.01 us

profile of v3, /device:TPU:1, one launch (start us, length us, event | category | flops | bytes accessed | tf_op | source)
XLA Modules:
  0.0 270.8 jit_solution(13798769286918343172)
XLA Ops:
  0.0 0.7 reduce_sum.27
  0.8 0.1 pad.6.clone
  0.8 0.7 fusion.10
  1.5 0.7 fusion.12
  2.2 0.7 maximum_maximum_fusion.table_ref
  2.9 10.2 %local_terms.1 = (bf16[16,272,128]{2,1,0:T(8,128)(2,1)}, bf16[16,128,128]{2,1,0:T(8,128)(2,1)}, f32[16,128,128]{2,1,0:T(8,128)}) custom-call(bf16[128,1024]{1,0:T(8,128)(2,1)} %bitcast.51, bf16[128,1024]{1,0:T(8,128)(2,1)} %bitcast.52, bf16[128,2048]{1,0:T(8,128)(2,1)} %bitcast.50, f32[2,8,128]{2,1,0:T(8,128)} %bitcast.53, f32[2,8,128]{2,1,0:T(8,128)} %bitcast.54), custom_call_target="tpu_custom_call" | custom-call | tf_op jit(solution)/shard_map/local_terms/pallas_call | solution.py:112
  13.1 31.8 %prefix.1 = (bf16[16,128,128]{2,1,0:T(8,128)(2,1)}, bf16[3,4,32,128]{3,2,1,0:T(8,128)(2,1)}) custom-call(bf16[16,272,128]{2,1,0:T(8,128)(2,1)} %get-tuple-element.20.map_ref, bf16[32,128]{1,0:T(8,128)(2,1)} %maximum_maximum_fusion.table_ref), custom_call_target="tpu_custom_call" | custom-call | tf_op jit(solution)/shard_map/prefix/pallas_call | solution.py:306
  44.9 0.0 copy-start
  44.9 8.0 %finish.1 = (f32[128,2048]{1,0:T(8,128)}, bf16[128,768]{1,0:T(8,128)(2,1)}, bf16[128,640]{1,0:T(8,128)(2,1)}, bf16[128,640]{1,0:T(8,128)(2,1)}) custom-call(bf16[16,128,128]{2,1,0:T(8,128)(2,1)} %get-tuple-element.22.state_ref, bf16[16,128,128]{2,1,0:T(8,128)(2,1)} %get-tuple-element.23.reader_ref, f32[16,128,128]{2,1,0:T(8,128)} %get-tuple-element.24.local_ref, ...), custom_call_target="tpu_custom_call" | custom-call | tf_op jit(solution)/shard_map/finish/pallas_call | solution.py:364
  52.9 0.0 copy-done
  52.9 0.8 fusion.1
  53.7 1.1 copy.21.refs_1_
  54.8 0.2 fusion.2
  55.0 1.4 compare_select_fusion.1.refs_0_
  56.4 95.5 %dispatch.1 = (bf16[32,4,16,768]{3,2,1,0:T(8,128)(2,1)}, bf16[32,4,16,640]{3,2,1,0:T(8,128)(2,1)}, bf16[32,4,16,640]{3,2,1,0:T(8,128)(2,1)}) custom-call(f32[3,32,4,2,128]{4,3,2,1,0:T(2,128)} %compare_select_fusion.1.refs_0_, bf16[128,768]{1,0:T(8,128)(2,1)} %get-tuple-element.26.refs_1_, bf16[128,640]{1,0:T(8,128)(2,1)} %get-tuple-element.27.refs_2_, ...), custom_call_target="tpu_custom_call" | custom-call | tf_op jit(solution)/shard_map/dispatch/pallas_call | solution.py:460
  151.9 21.2 %experts.1 = (bf16[4,4,2,4,16,768]{5,4,3,2,1,0:T(8,128)(2,1)}, bf16[4,4,2,4,16,640]{5,4,3,2,1,0:T(8,128)(2,1)}, bf16[4,4,2,4,16,640]{5,4,3,2,1,0:T(8,128)(2,1)}) custom-call(bf16[4,4,2,4,16,768]{5,4,3,2,1,0:T(8,128)(2,1)} %bitcast.41, bf16[4,4,2,4,16,640]{5,4,3,2,1,0:T(8,128)(2,1)} %bitcast.43, bf16[4,4,2,4,16,640]{5,4,3,2,1,0:T(8,128)(2,1)} %bitcast.44, ...), custom_call_target="tpu_custom_call" | custom-call | tf_op jit(solution)/shard_map/experts/pallas_call | solution.py:581
  173.1 95.9 %collect.1 = bf16[128,2048]{1,0:T(8,128)(2,1)} custom-call(f32[3,32,4,2,128]{4,3,2,1,0:T(2,128)} %compare_select_fusion.1.refs_0_, f32[3,32,4,2,128]{4,3,2,1,0:T(2,128)} %copy.21.refs_1_, f32[128,2048]{1,0:T(8,128)} %get-tuple-element.25.refs_2_, bf16[32,4,16,768]{3,2,1,0:T(8,128)(2,1)} %bitcast.42, bf16[32,4,16,640]{3,2,1,0:T(8,128)(2,1)} %bitcast.45, ...), custom_call_target="tpu_custom_call" | custom-call | tf_op jit(solution)/shard_map/collect/pallas_call | solution.py:521
  269.0 1.9 copy.41
  (7 shorter events, 0.1 us)
Async XLA Ops:
  44.9 8.0 %copy-start = (bf16[3,4,32,128]{3,2,1,0:T(8,128)(2,1)S(1)}, bf16[3,4,32,128]{3,2,1,0:T(8,128)(2,1)}, u32[]{:S(2)}) copy-start(bf16[3,4,32,128]{3,2,1,0:T(8,128)(2,1)} %get-tuple-element.21) | copy-start | bytes 294916

commit v4 on v3

--- a/solution.py
+++ b/solution.py
@@ -420,88 +420,177 @@
     return slot[..., None, :] == rows
 
 
-def dispatch_kernel(*refs):
-    slot_ref, rows, outs = refs[0], refs[1:4], refs[4:7]
-    lines, stages = refs[7:10], refs[10:13]
-    line_semaphores, (send, receive) = refs[13:16], refs[16:18]
+def whole_copies(sources, targets, semaphores):
+    return [pltpu.make_async_copy(sources[part], targets[part], semaphores.at[part]) for part in range(3)]
+
+
+def expert_rows(step, buffers, x_ref):
+    a_ref, b_ref, c_ref = buffers
+    wa, wb = a_ref.shape[2], b_ref.shape[2]
+    pair, core = step // 2, step % 2
+    tile = pl.ds(pl.multiple_of(pair * 16, 16), 16)
+    parts_c = [[c_ref[(x * 4 + y) * 2 + core, tile].astype(F32) for y in range(4)] for x in range(4)]
+    for n in range(2):
+        z = pair * 2 + n
+        parts_b = [b_ref[(z * 4 + y) * 2 + core].astype(F32) for y in range(4)]
+        for x in range(4):
+            rows = slice((n * 4 + x) * 32, (n * 4 + x) * 32 + 32)
+            x_ref[rows, 0:wa] = a_ref[(z * 4 + x) * 2 + core]
+            x_ref[rows, wa:wa + wb] = jnp.concatenate(
+                [parts_b[y][x * ROWS:(x + 1) * ROWS] for y in range(4)], axis=0
+            ).astype(BF16)
+            x_ref[rows, wa + wb:] = jnp.concatenate(
+                [parts_c[x][y][n * ROWS:(n + 1) * ROWS] for y in range(4)], axis=0
+            ).astype(BF16)
+
+
+def expert_results(step, result, stages):
+    a_ref, b_ref, c_ref = stages
+    wa, wb = a_ref.shape[2], b_ref.shape[2]
+    pair, core = step // 2, step % 2
+    tile = pl.ds(pl.multiple_of(pair * 16, 16), 16)
+
+    def piece(n, x, y, low, high):
+        start = ((n * 4 + x) * 4 + y) * ROWS
+        return result[start:start + ROWS, low:high]
+
+    for n in range(2):
+        z = pair * 2 + n
+        for x in range(4):
+            start = (n * 4 + x) * 32
+            a_ref[(z * 4 + x) * 2 + core] = result[start:start + 32, 0:wa].astype(BF16)
+        for y in range(4):
+            b_ref[(z * 4 + y) * 2 + core] = jnp.concatenate(
+                [piece(n, x, y, wa, wa + wb) for x in range(4)], axis=0
+            ).astype(BF16)
+    for x in range(4):
+        for y in range(4):
+            c_ref[(x * 4 + y) * 2 + core, tile] = jnp.concatenate(
+                [piece(n, x, y, wa + wb, result.shape[1]) for n in range(2)], axis=0
+            ).astype(BF16)
+
+
+def moe_kernel(*refs):
+    slot_ref, share_ref, mid_ref, rows, up_ref, down_ref = refs[0], refs[1], refs[2], refs[3:6], refs[6], refs[7]
+    out_ref, arrived, returned = refs[8], refs[9:12], refs[12:15]
+    lines, stages, buffers, sums, totals = refs[15:18], refs[18:21], refs[21:24], refs[24:27], refs[27:30]
+    up_v, down_v, x_ref = refs[30:33]
+    gather_semaphores, scatter_semaphores = refs[33:36], refs[36:39]
+    send, receive, send_back, receive_back, load, fetch = refs[39:45]
+    hidden_width = down_ref.shape[1]
+
+    def weight_copies(j):
+        return (
+            pltpu.make_async_copy(up_ref.at[j], up_v, fetch.at[0]),
+            pltpu.make_async_copy(down_ref.at[j], down_v, fetch.at[1]),
+        )
+
+    weights = weight_copies(0)
+    for copy in weights:
+        copy.start()
     greet(plane_offsets())
-    gathers = line_copies(rows, lines, line_semaphores, False)
+    gathers = line_copies(rows, lines, gather_semaphores, False)
     for copy in gathers:
         copy.start()
     for copy in gathers:
         copy.wait()
-    copies = []
-    for g in range(4):
-        steps = ORDER[8 * g:8 * g + 8]
-        for part in range(3):
-            places = [plane_index(part, across(part, *step)) for step in steps]
-
-            def fill(a, carry, part=part, places=places, g=g):
-                slots = jnp.concatenate([slot_ref[part, place, a] for place in places], axis=0)
-                take = jnp.where(picked(slots), 1.0, 0.0).reshape(16 * ROWS, TOK).astype(BF16)
-                packed = mul(take, lines[part][a]).astype(BF16)
-                stages[part][8 * g:8 * g + 8, a] = packed.reshape(8, 2 * ROWS, packed.shape[1])
-                return carry
-
-            lax.fori_loop(0, 4, fill, 0)
-            here = plane_index(part, (0, 0, 0, 0))
-            for i, step in enumerate(steps):
-                copy = plane_copy(stages[part].at[8 * g + i], outs[part].at[here], send, receive, part, step)
+
+    out_copies = []
+    for j in range(2):
+        copies = []
+        for g in range(2):
+            steps = ORDER[16 * g:16 * g + 16]
+            for part in range(3):
+                places = [plane_index(part, across(part, *step)) for step in steps]
+
+                def fill(pair, carry, part=part, places=places, g=g, j=j):
+                    packed = []
+                    for n in range(2):
+                        a = pair * 2 + n
+                        slots = jnp.concatenate([slot_ref[part, place, a, j:j + 1] for place in places], axis=0)
+                        take = jnp.where(picked(slots), 1.0, 0.0).reshape(16 * ROWS, TOK).astype(BF16)
+                        packed.append(mul(take, lines[part][a]).reshape(16, ROWS, lines[part].shape[2]))
+                    tile = pl.ds(pl.multiple_of(pair * 16, 16), 16)
+                    stages[part][j, 16 * g:16 * g + 16, tile] = jnp.concatenate(packed, axis=1).astype(BF16)
+                    return carry
+
+                lax.fori_loop(0, 2, fill, 0)
+                here = plane_index(part, (0, 0, 0, 0))
+                for i, step in enumerate(steps):
+                    copy = plane_copy(
+                        stages[part].at[j, 16 * g + i], arrived[part].at[j, here],
+                        send.at[j], receive.at[j], part, step,
+                    )
+                    copy.start()
+                    copies.append((copy, step))
+        out_copies.append(copies)
+
+    back_copies = []
+    for j in range(2):
+        for copy, step in out_copies[j]:
+            wait_arrived(copy, step)
+        loads = whole_copies([ref.at[j] for ref in arrived], buffers, load)
+        for copy in loads:
+            copy.start()
+        for copy, step in out_copies[j]:
+            wait_sent(copy, step)
+        for copy in weights:
+            copy.wait()
+        for copy in loads:
+            copy.wait()
+
+        def expert_step(step, carry, j=j):
+            expert_rows(step, buffers, x_ref)
+            both = mul(x_ref[...], up_v[...])
+            gate = both[:, :hidden_width]
+            hidden = (gate / (1.0 + jnp.exp(-gate)) * both[:, hidden_width:]).astype(BF16)
+            expert_results(step, mul(hidden, down_v[...]), [ref.at[j] for ref in stages])
+            return carry
+
+        lax.fori_loop(0, 4, expert_step, 0)
+        if j == 0:
+            weights = weight_copies(1)
+            for copy in weights:
+                copy.start()
+        copies = []
+        for step in ORDER:
+            for part in range(3):
+                copy = plane_copy(
+                    stages[part].at[j, plane_index(part, across(part, *step))],
+                    returned[part].at[j, plane_index(part, (0, 0, 0, 0))],
+                    send_back.at[j], receive_back.at[j], part, step,
+                )
                 copy.start()
                 copies.append((copy, step))
-    for copy, step in copies:
-        wait_sent(copy, step)
-        wait_arrived(copy, step)
-
-
-def dispatch(slots, rows):
-    dma = pltpu.SemaphoreType.DMA
-    shapes = [(32, 4, 2 * ROWS, part.shape[1]) for part in rows]
-    return pl.pallas_call(
-        dispatch_kernel,
-        in_specs=[pl.BlockSpec(memory_space=pltpu.VMEM)] * 4,
-        out_specs=[pl.BlockSpec(memory_space=pl.ANY)] * 3,
-        out_shape=[jax.ShapeDtypeStruct(shape, BF16) for shape in shapes],
-        scratch_shapes=[pltpu.VMEM((4,) + part.shape, BF16) for part in rows]
-        + [pltpu.VMEM(shape, BF16) for shape in shapes]
-        + [dma((3, 4)), dma((3, 4)), dma((3,)), dma((3, 32)), dma((3, 32))],
-        compiler_params=pltpu.CompilerParams(
-            collective_id=1, has_side_effects=True, vmem_limit_bytes=VMEM
-        ),
-        name="dispatch",
-    )(slots, *rows)
-
-
-def collect_kernel(*refs):
-    slot_ref, share_ref, mid_ref, results, out_ref = refs[0], refs[1], refs[2], refs[3:6], refs[6]
-    landed, partials, sums = refs[7:10], refs[10:13], refs[13:16]
-    send, receive = refs[16:18]
-    line_semaphores = refs[18:21]
-    greet(plane_offsets())
-    copies = [[], [], []]
-    for step in ORDER:
+        back_copies.append(copies)
+
+    scatters = line_copies(lines, sums, scatter_semaphores, True)
+    own, others = scatters[0:3], scatters[3:]
+    row = lax.broadcasted_iota(jnp.int32, (2 * ROWS, TOK), 0).astype(F32)
+    for j in range(2):
+        for copy, step in back_copies[j]:
+            wait_arrived(copy, step)
+        loads = whole_copies([ref.at[j] for ref in returned], buffers, load)
+        for copy in loads:
+            copy.start()
         for part in range(3):
-            target = landed[part].at[plane_index(part, (0, 0, 0, 0))]
-            source = results[part].at[plane_index(part, across(part, *step))]
-            copy = plane_copy(source, target, send, receive, part, step)
-            copy.start()
-            copies[part].append((copy, step))
-    lines = line_copies(partials, sums, line_semaphores, True)
-    own, others = lines[0:3], lines[3:]
-    for part in range(3):
-        for copy, step in copies[part]:
-            wait_arrived(copy, step)
-        width = landed[part].shape[3]
-        for n, d in enumerate((1, 3, 2, 0)):
-            a = lax.rem(line_place(part) + d, 4)
-            slot = slot_ref[part, :, a]
-            give = jnp.where(picked(slot), share_ref[part, :, a][:, :, None, :], 0.0)
-            high, low = halves(give.reshape(64 * ROWS, TOK))
-            rows = landed[part][:, a].reshape(64 * ROWS, width)
-            both = mul(jnp.concatenate([high, low], axis=1), rows, TN)
-            partials[part][a] = (both[:TOK] + both[TOK:]).astype(BF16)
-            copy = own[part] if d == 0 else others[3 * n + part]
-            copy.start()
+            loads[part].wait()
+            width = buffers[part].shape[2]
+            for n, d in enumerate((1, 3, 2, 0)):
+                a = lax.rem(line_place(part) + d, 4)
+                tile = pl.ds(pl.multiple_of(a // 2 * 16, 16), 16)
+                shift = (a % 2 * ROWS).astype(F32)
+                slots = slot_ref[part, :, a, j] + shift
+                give = jnp.where(slots[:, None, :] == row, share_ref[part, :, a, j][:, None, :], 0.0)
+                high, low = halves(give.reshape(64 * ROWS, TOK))
+                values = buffers[part][:, tile].reshape(64 * ROWS, width)
+                both = mul(jnp.concatenate([high, low], axis=1), values, TN)
+                if j == 0:
+                    totals[part][a] = both[:TOK] + both[TOK:]
+                else:
+                    lines[part][a] = (totals[part][a] + both[:TOK] + both[TOK:]).astype(BF16)
+                    copy = own[part] if d == 0 else others[3 * n + part]
+                    copy.start()
     for part, (low, high) in enumerate(PARTS):
         for n in range(3):
             others[3 * n + part].wait()
@@ -510,88 +599,34 @@
         for a in range(4):
             total = total + sums[part][a].astype(F32)
         out_ref[:, low:high] = total.astype(BF16)
-    for part in range(3):
-        for copy, step in copies[part]:
+    for copies in back_copies:
+        for copy, step in copies:
             wait_sent(copy, step)
 
 
-def collect(slots, shares, mid, results):
+def moe(slots, shares, mid, rows, up, down):
     dma = pltpu.SemaphoreType.DMA
-    widths = [part.shape[3] for part in results]
+    widths = [part.shape[1] for part in rows]
+    exchange = [jax.ShapeDtypeStruct((2, 32, 4 * ROWS, width), BF16) for width in widths]
     return pl.pallas_call(
-        collect_kernel,
-        in_specs=[pl.BlockSpec(memory_space=pltpu.VMEM)] * 3 + [pl.BlockSpec(memory_space=pl.ANY)] * 3,
-        out_specs=pl.BlockSpec(memory_space=pltpu.VMEM),
-        out_shape=jax.ShapeDtypeStruct(mid.shape, BF16),
-        scratch_shapes=[pltpu.VMEM(part.shape, BF16) for part in results]
-        + [pltpu.VMEM((4, TOK, width), BF16) for width in widths] * 2
-        + [dma((3, 32)), dma((3, 32)), dma((3, 4)), dma((3, 4)), dma((3,))],
+        moe_kernel,
+        in_specs=[pl.BlockSpec(memory_space=pltpu.VMEM)] * 6 + [pl.BlockSpec(memory_space=pl.ANY)] * 2,
+        out_specs=[pl.BlockSpec(memory_space=pltpu.VMEM)] + [pl.BlockSpec(memory_space=pl.ANY)] * 6,
+        out_shape=[jax.ShapeDtypeStruct(mid.shape, BF16)] + exchange + exchange,
+        scratch_shapes=[pltpu.VMEM((4, TOK, width), BF16) for width in widths]
+        + [pltpu.VMEM((2, 32, 4 * ROWS, width), BF16) for width in widths]
+        + [pltpu.VMEM((32, 4 * ROWS, width), BF16) for width in widths]
+        + [pltpu.VMEM((4, TOK, width), BF16) for width in widths]
+        + [pltpu.VMEM((4, TOK, width), F32) for width in widths]
+        + [pltpu.VMEM(up.shape[1:], BF16), pltpu.VMEM(down.shape[1:], BF16), pltpu.VMEM((256, up.shape[1]), BF16)]
+        + [dma((3, 4)), dma((3, 4)), dma((3,))] * 2
+        + [dma((2, 3, 32))] * 4
+        + [dma((3,)), dma((2,))],
         compiler_params=pltpu.CompilerParams(
-            collective_id=2, has_side_effects=True, vmem_limit_bytes=VMEM
+            collective_id=1, has_side_effects=True, vmem_limit_bytes=VMEM
         ),
-        name="collect",
-    )(slots, shares, mid, *results)
-
-
-def part_views(parts):
-    a, b, c = parts
-    return (
-        a.reshape(4, 4, 2, 4, 2 * ROWS, a.shape[3]),
-        b.reshape(4, 4, 2, 4, 2 * ROWS, b.shape[3]),
-        c.reshape(4, 4, 2, 4, 2 * ROWS, c.shape[3]),
-    )
-
-
-def expert_kernel(a_ref, b_ref, c_ref, up_ref, down_ref, ya_ref, yb_ref, yc_ref, x_ref, y_ref):
-    hidden_width = down_ref.shape[1]
-    wa, wb = a_ref.shape[5], b_ref.shape[5]
-    width = x_ref.shape[2]
-    sources = [(x * 8 + core * 4 + y, x, core, y) for x in range(4) for core in range(2) for y in range(4)]
-    for n, x, core, y in sources:
-        x_ref[n, :, 0:wa] = a_ref[0, x, core, y]
-        x_ref[n, :, wa:wa + wb] = b_ref[0, y, core, x]
-        x_ref[n, :, wa + wb:] = c_ref[x, y, core, 0]
-    rows = len(sources) * ROWS
-    x_all = x_ref[...].astype(F32)
-    results = []
-    for j in range(2):
-        mine = x_all[:, j * ROWS:(j + 1) * ROWS].reshape(rows, width).astype(BF16)
-        gate = mul(mine, up_ref[j, :, :hidden_width])
-        lift = mul(mine, up_ref[j, :, hidden_width:])
-        hidden = (gate / (1.0 + jnp.exp(-gate)) * lift).astype(BF16)
-        results.append(mul(hidden, down_ref[j]).reshape(len(sources), ROWS, width))
-    y_ref[...] = jnp.concatenate(results, axis=1).astype(BF16)
-    for n, x, core, y in sources:
-        ya_ref[0, x, core, y] = y_ref[n, :, 0:wa]
-        yb_ref[0, y, core, x] = y_ref[n, :, wa:wa + wb]
-        yc_ref[x, y, core, 0] = y_ref[n, :, wa + wb:]
-
-
-def experts(parts, up, down):
-    views = part_views(parts)
-    width = up.shape[1]
-    whole3 = lambda z: (0, 0, 0)
-    first = lambda z: (z, 0, 0, 0, 0, 0)
-    last = lambda z: (0, 0, 0, z, 0, 0)
-    specs = [
-        pl.BlockSpec((1,) + views[0].shape[1:], first),
-        pl.BlockSpec((1,) + views[1].shape[1:], first),
-        pl.BlockSpec(views[2].shape[:3] + (1,) + views[2].shape[4:], last),
-    ]
-    results = pl.pallas_call(
-        expert_kernel,
-        grid=(4,),
-        in_specs=specs + [
-            pl.BlockSpec(up.shape, whole3, pipeline_mode=pl.Buffered(1)),
-            pl.BlockSpec(down.shape, whole3, pipeline_mode=pl.Buffered(1)),
-        ],
-        out_specs=specs,
-        out_shape=[jax.ShapeDtypeStruct(view.shape, BF16) for view in views],
-        scratch_shapes=[pltpu.VMEM((32, 2 * ROWS, width), BF16), pltpu.VMEM((32, 2 * ROWS, width), BF16)],
-        compiler_params=pltpu.CompilerParams(vmem_limit_bytes=VMEM),
-        name="experts",
-    )(*views, up, down)
-    return [result.reshape(part.shape) for result, part in zip(results, parts)]
+        name="moe",
+    )(slots, shares, mid, *rows, up, down)[0]
 
 
 def routing_table(ids, weights):
@@ -647,9 +682,7 @@
         states, reader, local, gate_z[0], norm_gain, out_weight, residual[0], post_gain
     )
     slots, shares = routes(tables, expert_ids.shape[2], exp_dev)
-    arrived = dispatch(slots, rows)
-    results = experts(arrived, expert_up, expert_down)
-    return collect(slots, shares, mid, results)[None]
+    return moe(slots, shares, mid, rows, expert_up, expert_down)[None]
 
 
 def solution(mesh):

time: 271 us -> 238 us (0.88)
  Pallas kernels: 262 us -> 230 us
    pallas_call x3 -> x1, Pallas kernels: 213 us -> 180 us  [moe(): pl.pallas_call(moe_kernel, in_specs=[pl.BlockSpec(memory_space=pltpu.VMEM...]
where the time goes in v4:
time: 238 us
  Pallas kernels  230 us (97%)
  other arithmetic  5.06 us (2%)
  local copies, waits for them, and re-layouts  3.02 us (1%)
    pallas_call x1, Pallas kernels, moe(): pl.pallas_call(moe_kernel, in_specs=[pl.BlockSpec(memory_space=pltpu.VMEM...  180 us
    pallas_call x1, Pallas kernels, prefix(): pl.pallas_call(prefix_kernel, out_shape=[jax.ShapeDtypeStruct((HV, DK, DK...  31.8 us
    pallas_call x1, Pallas kernels, local_terms(): pl.pallas_call(local_kernel, grid=(GROUPS,), in_specs=[pl.BlockSpec((TOK,...  10.2 us
    pallas_call x1, Pallas kernels, finish(): pl.pallas_call(finish_kernel, grid=(width // tile,), in_specs=[pl.BlockSp...  8.03 us

profile of v4, /device:TPU:1, one launch (start us, length us, event | category | flops | bytes accessed | tf_op | source)
XLA Modules:
  0.0 238.0 jit_solution(6919905057889093975)
XLA Ops:
  0.0 0.7 reduce_sum.27
  0.8 0.1 pad.6.clone
  0.8 0.7 fusion.10
  1.5 0.7 fusion.12
  2.2 0.7 maximum_maximum_fusion.table_ref
  2.9 10.2 %local_terms.1 = (bf16[16,272,128]{2,1,0:T(8,128)(2,1)}, bf16[16,128,128]{2,1,0:T(8,128)(2,1)}, f32[16,128,128]{2,1,0:T(8,128)}) custom-call(bf16[128,1024]{1,0:T(8,128)(2,1)} %bitcast.39, bf16[128,1024]{1,0:T(8,128)(2,1)} %bitcast.40, bf16[128,2048]{1,0:T(8,128)(2,1)} %bitcast.37, f32[2,8,128]{2,1,0:T(8,128)} %bitcast.41, f32[2,8,128]{2,1,0:T(8,128)} %bitcast.42), custom_call_target="tpu_custom_call" | custom-call | tf_op jit(solution)/shard_map/local_terms/pallas_call | solution.py:112
  13.1 31.8 %prefix.1 = (bf16[16,128,128]{2,1,0:T(8,128)(2,1)}, bf16[3,4,32,128]{3,2,1,0:T(8,128)(2,1)}) custom-call(bf16[16,272,128]{2,1,0:T(8,128)(2,1)} %get-tuple-element.15.map_ref, bf16[32,128]{1,0:T(8,128)(2,1)} %maximum_maximum_fusion.table_ref), custom_call_target="tpu_custom_call" | custom-call | tf_op jit(solution)/shard_map/prefix/pallas_call | solution.py:306
  44.9 0.0 copy-start
  44.9 8.0 %finish.1 = (f32[128,2048]{1,0:T(8,128)}, bf16[128,768]{1,0:T(8,128)(2,1)}, bf16[128,640]{1,0:T(8,128)(2,1)}, bf16[128,640]{1,0:T(8,128)(2,1)}) custom-call(bf16[16,128,128]{2,1,0:T(8,128)(2,1)} %get-tuple-element.17.state_ref, bf16[16,128,128]{2,1,0:T(8,128)(2,1)} %get-tuple-element.18.reader_ref, f32[16,128,128]{2,1,0:T(8,128)} %get-tuple-element.19.local_ref, ...), custom_call_target="tpu_custom_call" | custom-call | tf_op jit(solution)/shard_map/finish/pallas_call | solution.py:364
  52.9 0.0 copy-done
  53.0 0.8 fusion.1
  53.8 1.1 copy.21.refs_1_
  54.8 0.2 fusion.2
  55.0 1.4 compare_select_fusion.1.refs_0_
  56.4 179.7 %moe.1 = (bf16[128,2048]{1,0:T(8,128)(2,1)}, bf16[2,32,32,768]{3,2,1,0:T(8,128)(2,1)}, bf16[2,32,32,640]{3,2,1,0:T(8,128)(2,1)}, bf16[2,32,32,640]{3,2,1,0:T(8,1...) custom-call(f32[3,32,4,2,128]{4,3,2,1,0:T(2,128)} %compare_select_fus, ...), custom_call_target="tpu_custom_call" | custom-call | tf_op jit(solution)/shard_map/moe/pallas_call | solution.py:611
  236.1 1.9 copy.41
  (7 shorter events, 0.1 us)
Async XLA Ops:
  44.9 8.0 %copy-start = (bf16[3,4,32,128]{3,2,1,0:T(8,128)(2,1)S(1)}, bf16[3,4,32,128]{3,2,1,0:T(8,128)(2,1)}, u32[]{:S(2)}) copy-start(bf16[3,4,32,128]{3,2,1,0:T(8,128)(2,1)} %get-tuple-element.16) | copy-start | bytes 294916

commit v5 on v4

v5 whole, which is shorter than its diff:
```python
import functools

import jax
import jax.numpy as jnp
from jax import lax
from jax.experimental import pallas as pl
from jax.experimental.pallas import tpu as pltpu
from jax.sharding import PartitionSpec as P

TOK = 128
DK = 128
HV = 16
HK = 8
GROUPS = 2
ROWS = 8
MSG = 272
VMEM = 60 << 20
PARTS = ((0, 768), (768, 1408), (1408, 2048))
MESH = pl.DeviceIdType.MESH
EPSILON = 1e-06
PRECISE = lax.Precision.HIGHEST
F32 = jnp.float32
BF16 = jnp.bfloat16

NN = (((1,), (0,)), ((), ()))
NT = (((1,), (1,)), ((), ()))
TN = (((0,), (0,)), ((), ()))


def mul(a, b, dims=NN):
    return lax.dot_general(a, b, dims, preferred_element_type=F32)


def mul_precise(a, b, dims=NN):
    return lax.dot_general(a, b, dims, preferred_element_type=F32, precision=PRECISE)


def halves(a):
    high = a.astype(BF16)
    return high, (a - high.astype(F32)).astype(BF16)


def axis_names():
    seq = lax.axis_index("seq")
    return (lax.div(seq, 8), lax.rem(lax.div(seq, 2), 4), lax.rem(seq, 2), lax.axis_index("batch"))


def device_at(offset):
    z, x, core, y = axis_names()
    dz, dx, dcore, dy = offset
    seq = lax.rem(z + dz, 4) * 8 + lax.rem(x + dx, 4) * 2 + lax.rem(core + dcore, 2)
    return (seq, lax.rem(y + dy, 4))


def greet(offsets):
    barrier = pltpu.get_barrier_semaphore()
    for offset in offsets:
        pl.semaphore_signal(barrier, inc=1, device_id=device_at(offset), device_id_type=MESH)
    pl.semaphore_wait(barrier, len(offsets))


def along(part, d):
    return ((0, 0, 0, d), (0, d, 0, 0), (d, 0, 0, 0))[part]


def across(part, p, q, dcore):
    return ((p, q, dcore, 0), (p, 0, dcore, q), (0, p, dcore, q))[part]


def line_place(part):
    z, x, _, y = axis_names()
    return (y, x, z)[part]


def plane_index(part, offset):
    z, x, core, y = axis_names()
    dz, dx, dcore, dy = offset
    z, x, y = lax.rem(z + dz, 4), lax.rem(x + dx, 4), lax.rem(y + dy, 4)
    first, second = ((z, x), (z, y), (x, y))[part]
    return (first * 4 + second) * 2 + lax.rem(core + dcore, 2)


PAIRS = (
    ((1, 1), (3, 3), (1, 3), (3, 1)),
    ((2, 2),),
    ((1, 0), (3, 0), (0, 1), (0, 3)),
    ((2, 0), (0, 2)),
    ((2, 1), (2, 3)),
    ((1, 2), (3, 2)),
)


def line_copies(sources, targets, semaphores, scatter):
    send, receive, own = semaphores
    copies = []
    for part in range(3):
        place = line_place(part)
        source = sources[part].at[place] if scatter else sources[part]
        copies.append(pltpu.make_async_copy(source, targets[part].at[place], own.at[part]))
    for d in (1, 3, 2):
        for part in range(3):
            place = line_place(part)
            source = sources[part].at[lax.rem(place + d, 4)] if scatter else sources[part]
            copies.append(pltpu.make_async_remote_copy(
                source, targets[part].at[place], send.at[part, d], receive.at[part, d],
                device_id=device_at(along(part, d)), device_id_type=MESH,
            ))
    return copies


def local_terms(g, q_ref, k_ref, v_ref, ld_ref, bt_ref, map_ref, reader_ref, local_ref, n_ref, x_ref, s_ref):
    heads = HV // GROUPS
    row = lax.broadcasted_iota(jnp.int32, (TOK, TOK), 0)
    col = lax.broadcasted_iota(jnp.int32, (TOK, TOK), 1)
    ld = ld_ref[g]
    cum_row = mul_precise(ld, (row <= col).astype(F32))
    cum_col = mul_precise((row >= col).astype(F32), ld, NT)
    beta_col = bt_ref[g].T
    units = []
    for pair in range(heads // 2):
        key_head = g * (heads // 2) + pair
        lanes = slice(key_head * DK, (key_head + 1) * DK)
        k_raw = k_ref[:, lanes]
        q_raw = q_ref[:, lanes]
        k_full = k_raw.astype(F32)
        q_full = q_raw.astype(F32)
        k_scale = lax.rsqrt(jnp.sum(k_full * k_full, axis=-1, keepdims=True) + EPSILON)
        q_scale = lax.rsqrt(jnp.sum(q_full * q_full, axis=-1, keepdims=True) + EPSILON) * DK ** (-0.5)
        k_unit = k_full * k_scale
        k_high, k_low = halves(k_unit)
        right = jnp.concatenate([k_high, k_low], axis=1)
        key_key = mul(jnp.concatenate([k_raw, k_raw], axis=1), right, NT) * k_scale
        query_key = mul(jnp.concatenate([q_raw, q_raw], axis=1), right, NT) * q_scale
        units.append((k_unit, q_full * q_scale))
        for h in (2 * pair, 2 * pair + 1):
            gap = cum_col[:, h:h + 1] - cum_row[h:h + 1, :]
            decay = jnp.where(row >= col, jnp.exp(jnp.minimum(gap, 0.0)), 0.0)
            s_ref[h] = (decay * query_key).astype(BF16)
            system = jnp.where(row > col, decay * key_key, 0.0) * beta_col[:, h:h + 1]
            n_ref[h] = system
            x_ref[h] = jnp.where((row ^ col) == 1, -system, 0.0)
    for level in range(1, 7):
        cross = ((row >> level) ^ (col >> level)) == 1
        left = []
        for h in range(heads):
            part = jnp.where(cross, n_ref[h], 0.0)
            left.append(part + mul(x_ref[h].astype(BF16), part.astype(BF16)))
        for h in range(heads):
            old = x_ref[h]
            x_ref[h] = old - left[h] - mul(left[h].astype(BF16), old.astype(BF16))
    line = lax.broadcasted_iota(jnp.int32, (16, DK), 0)
    for h in range(heads):
        k_unit, q_unit = units[h // 2]
        cum = cum_col[:, h:h + 1]
        last = cum_row[h:h + 1, TOK - 1:TOK]
        beta = beta_col[:, h:h + 1]
        gamma = jnp.exp(cum)
        head = g * heads + h
        value = v_ref[:, head * DK:(head + 1) * DK].astype(F32) * beta
        right = jnp.concatenate([value, k_unit * (beta * gamma)], axis=1)
        write = (right + mul(x_ref[h].astype(BF16), right.astype(BF16))).astype(BF16)
        tail = (jnp.exp(last - cum) * k_unit).astype(BF16)
        moved = mul(write, tail, TN)
        read = mul(s_ref[h], write)
        local_ref[head] = read[:, :DK]
        reader_ref[head] = (gamma * q_unit - read[:, DK:]).astype(BF16)
        whole = jnp.exp(jnp.broadcast_to(last, (16, DK)))
        part0 = whole.astype(BF16)
        part1 = (whole - part0.astype(F32)).astype(BF16)
        part2 = (whole - part0.astype(F32) - part1.astype(F32)).astype(BF16)
        parts = jnp.where(line == 0, part0.astype(F32), jnp.where(line == 1, part1.astype(F32), part2.astype(F32)))
        map_ref[head, 0:128] = (-moved[DK:]).astype(BF16)
        map_ref[head, 128:256] = moved[:DK].astype(BF16)
        map_ref[head, 256:272] = jnp.where(line < 3, parts, 0.0).astype(BF16)


def mixer_kernel(
    q_ref, k_ref, v_ref, ld_ref, bt_ref, gate_ref, gain_ref, resid_ref, post_ref, ids_hbm, scores_hbm, weight_ref,
    mid_ref, a_ref, b_ref, c_ref, tables_ref,
    map_ref, reader_ref, local_ref, n_ref, x_ref, s_ref, weight_v, normed_ref, state_ref, inbox, outbox, table_ref, ids_ref, scores_ref,
    send, receive, send_back, receive_back, fetch, *lines,
):
    seq, batch = lax.axis_index("seq"), lax.axis_index("batch")
    z, x, core = seq // 8, seq // 2 % 4, seq % 2
    count = inbox.shape[0]
    heads = HV // GROUPS
    owned = (z + x) % 2 * heads + z * 2 + x // 2

    weights = pltpu.make_async_copy(weight_ref, weight_v, fetch.at[0])
    routing = (
        pltpu.make_async_copy(ids_hbm, ids_ref, fetch.at[1]),
        pltpu.make_async_copy(scores_hbm, scores_ref, fetch.at[2]),
    )
    for copy in routing:
        copy.start()
    weights.start()
    barrier = pltpu.get_barrier_semaphore()
    for other in range(1, count):
        pl.semaphore_signal(
            barrier, inc=1, device_id=(lax.rem(seq + other, count), batch), device_id_type=MESH
        )
    for d in (1, 2, 3):
        pl.semaphore_signal(barrier, inc=1, device_id=device_at((0, 0, 0, d)), device_id_type=MESH)

    def to_owner(g, n):
        i = lax.rem(n + z * 4 + x, heads)
        head = g * heads + i
        to_z = i // 2
        owner = (to_z * 4 + i % 2 * 2 + (to_z + g) % 2) * 2
        remote = pltpu.make_async_remote_copy(
            map_ref.at[head], inbox.at[seq], send.at[head], receive.at[seq],
            device_id=(owner, batch), device_id_type=MESH,
        )
        own = pltpu.make_async_copy(map_ref.at[head], inbox.at[seq], receive.at[seq])
        return owner, remote, own

    def ship(g):
        for n in range(heads):
            owner, remote, own = to_owner(g, n)

            @pl.when(owner == seq)
            def _():
                own.start()

            @pl.when(owner != seq)
            def _():
                remote.start()

    local_args = (q_ref, k_ref, v_ref, ld_ref, bt_ref, map_ref, reader_ref, local_ref, n_ref, x_ref, s_ref)
    local_terms(0, *local_args)
    pl.semaphore_wait(barrier, count + 2)
    ship(0)
    for copy in routing:
        copy.wait()
    top = ids_ref.shape[0]
    numbers = jnp.concatenate([ids_ref[k] for k in range(top)], axis=0).astype(F32)
    scores = jnp.concatenate([scores_ref[k] for k in range(top)], axis=0)
    high, low = halves(scores / jnp.sum(scores, axis=0, keepdims=True))
    spare = jnp.zeros((16 - numbers.shape[0], TOK), F32)
    for n, value in enumerate((numbers, high.astype(F32), low.astype(F32))):
        table_ref[16 * n:16 * n + 16] = jnp.concatenate([value, spare], axis=0).astype(BF16)
    tables = line_copies((table_ref,) * 3, [tables_ref.at[part] for part in range(3)], lines, False)
    for copy in tables:
        copy.start()
    local_terms(1, *local_args)
    ship(1)

    def back(place):
        return pltpu.make_async_remote_copy(
            outbox.at[place], state_ref.at[owned], send_back.at[place], receive_back.at[owned],
            device_id=(place, batch), device_id_type=MESH,
        )

    @pl.when(core == 0)
    def _():
        def step(place, state):
            pltpu.make_async_copy(inbox.at[place], inbox.at[place], receive.at[place]).wait()
            high, low = halves(state)
            outbox[place] = high

            @pl.when(place == seq)
            def _():
                pltpu.make_async_copy(outbox.at[seq], state_ref.at[owned], receive_back.at[owned]).start()

            @pl.when(place != seq)
            def _():
                back(place).start()

            both = mul(jnp.concatenate([high, low], axis=0), inbox[place, 0:128])
            parts = inbox[place, 256:272].astype(F32)
            gamma = parts[0:1] + parts[1:2] + parts[2:3]
            return state * gamma + (both[:DK] + both[DK:]) + inbox[place, 128:256].astype(F32)

        lax.fori_loop(0, count, step, jnp.zeros((DK, DK), F32))

    for h in range(HV):
        pltpu.make_async_copy(state_ref.at[h], state_ref.at[h], receive_back.at[h]).wait()
        kept = mul(reader_ref[h], state_ref[h], NT) + local_ref[h]
        scaled = kept * lax.rsqrt(jnp.mean(kept * kept, axis=-1, keepdims=True) + EPSILON)
        gate = gate_ref[:, h * DK:(h + 1) * DK].astype(F32)
        normed_ref[:, h * DK:(h + 1) * DK] = (
            scaled * gain_ref[...] * (gate / (1.0 + jnp.exp(-gate)))
        ).astype(BF16)
    weights.wait()
    width = mid_ref.shape[1]
    tile = 512
    total = jnp.zeros((TOK, 1), F32)
    for start in range(0, width, tile):
        lanes = slice(start, start + tile)
        mid = resid_ref[:, lanes].astype(F32) + mul(normed_ref[...], weight_v[:, lanes])
        mid_ref[:, lanes] = mid
        total = total + jnp.sum(mid * mid, axis=-1, keepdims=True)
    scale = lax.rsqrt(total / width + EPSILON)
    for ref, (low, high) in zip((a_ref, b_ref, c_ref), PARTS):
        ref[...] = (mid_ref[:, low:high] * scale * post_ref[:, low:high]).astype(BF16)

    for g in range(GROUPS):
        for n in range(heads):
            owner, remote, _ = to_owner(g, n)

            @pl.when(owner != seq)
            def _():
                remote.wait_send()

    @pl.when(core == 0)
    def _():
        def sent(place, carry):
            @pl.when(place != seq)
            def _():
                back(place).wait_send()

            return carry

        lax.fori_loop(0, count, sent, 0)

    for copy in tables:
        copy.wait()


def mixer(query, key, value, log_decay, strength, gate, gain, resid, post, ids, scores, weight, count):
    heads = HV // GROUPS
    width = weight.shape[1]
    dma = pltpu.SemaphoreType.DMA
    vmem = pltpu.VMEM
    return pl.pallas_call(
        mixer_kernel,
        in_specs=[pl.BlockSpec(memory_space=vmem)] * 9 + [pl.BlockSpec(memory_space=pl.ANY)] * 3,
        out_specs=[pl.BlockSpec(memory_space=vmem)] * 5,
        out_shape=[jax.ShapeDtypeStruct((TOK, width), F32)]
        + [jax.ShapeDtypeStruct((TOK, high - low), BF16) for low, high in PARTS]
        + [jax.ShapeDtypeStruct((3, 4, 48, TOK), BF16)],
        scratch_shapes=[
            vmem((HV, MSG, DK), BF16),
            vmem((HV, TOK, DK), BF16),
            vmem((HV, TOK, DK), F32),
            vmem((heads, TOK, TOK), F32),
            vmem((heads, TOK, TOK), F32),
            vmem((heads, TOK, TOK), BF16),
            vmem(weight.shape, BF16),
            vmem((TOK, weight.shape[0]), BF16),
            vmem((HV, DK, DK), BF16),
            vmem((count, MSG, DK), BF16),
            vmem((count, DK, DK), BF16),
            vmem((48, TOK), BF16),
            vmem(ids.shape, jnp.int32),
            vmem(scores.shape, F32),
            dma((HV,)),
            dma((count,)),
            dma((count,)),
            dma((HV,)),
            dma((3,)),
            dma((3, 4)),
            dma((3, 4)),
            dma((3,)),
        ],
        compiler_params=pltpu.CompilerParams(
            collective_id=0, has_side_effects=True, vmem_limit_bytes=VMEM
        ),
        name="mixer",
    )(
        query, key, value, log_decay.reshape(GROUPS, heads, TOK), strength.reshape(GROUPS, heads, TOK),
        gate, gain[None], resid, post[None], ids, scores, weight,
    )


ORDER = [(p, q, dcore) for group in PAIRS for dcore in (0, 1) for p, q in group] + [(0, 0, 1), (0, 0, 0)]


def plane_copy(source, target, send, receive, part, step):
    p, q, dcore = step
    offset = across(part, p, q, dcore)
    slot = p * 8 + q * 2 + dcore
    if step == (0, 0, 0):
        return pltpu.make_async_copy(source, target, receive.at[part, slot])
    return pltpu.make_async_remote_copy(
        source, target, send.at[part, slot], receive.at[part, slot],
        device_id=device_at(offset), device_id_type=MESH,
    )


def wait_sent(copy, step):
    if step != (0, 0, 0):
        copy.wait_send()


def wait_arrived(copy, step):
    if step == (0, 0, 0):
        copy.wait()
    else:
        copy.wait_recv()


def plane_offsets():
    return sorted(set(across(part, *step) for part in range(3) for step in ORDER) - {(0, 0, 0, 0)})


def picked(slot):
    rows = lax.broadcasted_iota(jnp.int32, (ROWS, TOK), 0).astype(F32)
    return slot[..., None, :] == rows


def whole_copies(sources, targets, semaphores):
    return [pltpu.make_async_copy(sources[part], targets[part], semaphores.at[part]) for part in range(3)]


def expert_rows(step, buffers, x_ref):
    a_ref, b_ref, c_ref = buffers
    wa, wb = a_ref.shape[2], b_ref.shape[2]
    pair, core = step // 2, step % 2
    tile = pl.ds(pl.multiple_of(pair * 16, 16), 16)
    parts_c = [[c_ref[(x * 4 + y) * 2 + core, tile].astype(F32) for y in range(4)] for x in range(4)]
    for n in range(2):
        z = pair * 2 + n
        parts_b = [b_ref[(z * 4 + y) * 2 + core].astype(F32) for y in range(4)]
        for x in range(4):
            rows = slice((n * 4 + x) * 32, (n * 4 + x) * 32 + 32)
            x_ref[rows, 0:wa] = a_ref[(z * 4 + x) * 2 + core]
            x_ref[rows, wa:wa + wb] = jnp.concatenate(
                [parts_b[y][x * ROWS:(x + 1) * ROWS] for y in range(4)], axis=0
            ).astype(BF16)
            x_ref[rows, wa + wb:] = jnp.concatenate(
                [parts_c[x][y][n * ROWS:(n + 1) * ROWS] for y in range(4)], axis=0
            ).astype(BF16)


def expert_results(step, result, stages):
    a_ref, b_ref, c_ref = stages
    wa, wb = a_ref.shape[2], b_ref.shape[2]
    pair, core = step // 2, step % 2
    tile = pl.ds(pl.multiple_of(pair * 16, 16), 16)

    def piece(n, x, y, low, high):
        start = ((n * 4 + x) * 4 + y) * ROWS
        return result[start:start + ROWS, low:high]

    for n in range(2):
        z = pair * 2 + n
        for x in range(4):
            start = (n * 4 + x) * 32
            a_ref[(z * 4 + x) * 2 + core] = result[start:start + 32, 0:wa].astype(BF16)
        for y in range(4):
            b_ref[(z * 4 + y) * 2 + core] = jnp.concatenate(
                [piece(n, x, y, wa, wa + wb) for x in range(4)], axis=0
            ).astype(BF16)
    for x in range(4):
        for y in range(4):
            c_ref[(x * 4 + y) * 2 + core, tile] = jnp.concatenate(
                [piece(n, x, y, wa + wb, result.shape[1]) for n in range(2)], axis=0
            ).astype(BF16)


def fill_slots(tables_ref, slot_ref, share_ref, top):
    z, x, _, y = axis_names()
    line = lax.broadcasted_iota(jnp.int32, (64, TOK), 0)
    half, place = line // 32, line % 32
    first, second, side = place // 8, place // 2 % 4, place % 2
    device = (
        place * 4 + y,
        (first * 8 + x * 2 + side) * 4 + second,
        (z * 8 + first * 2 + side) * 4 + second,
    )
    row = lax.broadcasted_iota(jnp.int32, (TOK, TOK), 0)
    col = lax.broadcasted_iota(jnp.int32, (TOK, TOK), 1)
    earlier = (row < col).astype(F32).astype(BF16)
    for part in range(3):
        expert = (device[part] * 2 + half).astype(F32)
        for a in range(4):
            table = tables_ref[part, a].astype(F32)
            chosen = jnp.zeros((64, TOK), F32)
            given = jnp.zeros((64, TOK), F32)
            for k in range(top):
                named = table[k:k + 1] == expert
                share = table[16 + k:17 + k] + table[32 + k:33 + k]
                chosen = jnp.where(named, 1.0, chosen)
                given = jnp.where(named, share, given)
            rank = mul(chosen.astype(BF16), earlier)
            slot_ref[part, a] = jnp.where(chosen > 0, rank, -1.0)
            share_ref[part, a] = given


def moe_kernel(top, *refs):
    tables_ref, mid_ref, rows, up_ref, down_ref = refs[0], refs[1], refs[2:5], refs[5], refs[6]
    out_ref, arrived, returned, staged = refs[7], refs[8:11], refs[11:14], refs[14:17]
    lines, stages, buffers, sums, totals = refs[17:20], refs[20:23], refs[23:26], refs[26:29], refs[29:32]
    up_v, down_v, x_ref, slot_ref, share_ref = refs[32:37]
    gather_semaphores, scatter_semaphores = refs[37:40], refs[40:43]
    send, receive, send_back, receive_back, load, fetch, store = refs[43:50]
    hidden_width = down_ref.shape[1]

    def weight_copies(j):
        return (
            pltpu.make_async_copy(up_ref.at[j], up_v, fetch.at[0]),
            pltpu.make_async_copy(down_ref.at[j], down_v, fetch.at[1]),
        )

    weights = weight_copies(0)
    for copy in weights:
        copy.start()
    greet(plane_offsets())
    gathers = line_copies(rows, lines, gather_semaphores, False)
    for copy in gathers:
        copy.start()
    fill_slots(tables_ref, slot_ref, share_ref, top)
    for copy in gathers:
        copy.wait()

    out_copies = []
    for j in range(2):
        copies = []
        for g in range(2):
            steps = ORDER[16 * g:16 * g + 16]
            group = slice(16 * g, 16 * g + 16)
            stores = []
            for part in range(3):
                places = [plane_index(part, across(part, *step)) for step in steps]

                def fill(pair, carry, part=part, places=places, group=group, j=j):
                    packed = []
                    for n in range(2):
                        a = pair * 2 + n
                        slots = jnp.concatenate(
                            [slot_ref[part, a, pl.ds(place + 32 * j, 1)] for place in places], axis=0
                        )
                        take = jnp.where(picked(slots), 1.0, 0.0).reshape(16 * ROWS, TOK).astype(BF16)
                        packed.append(mul(take, lines[part][a]).reshape(16, ROWS, lines[part].shape[2]))
                    tile = pl.ds(pl.multiple_of(pair * 16, 16), 16)
                    stages[part][j, group, tile] = jnp.concatenate(packed, axis=1).astype(BF16)
                    return carry

                lax.fori_loop(0, 2, fill, 0)
                stores.append(pltpu.make_async_copy(
                    stages[part].at[j, group], staged[part].at[j, group], store.at[part]
                ))
                stores[part].start()
            for copy in stores:
                copy.wait()
            for i, step in enumerate(steps):
                for part in range(3):
                    here = plane_index(part, (0, 0, 0, 0))
                    copy = plane_copy(
                        staged[part].at[j, 16 * g + i], arrived[part].at[j, here],
                        send.at[j], receive.at[j], part, step,
                    )
                    copy.start()
                    copies.append((copy, step))
        out_copies.append(copies)

    back_copies = []
    for j in range(2):
        for copy, step in out_copies[j]:
            wait_arrived(copy, step)
        loads = whole_copies([ref.at[j] for ref in arrived], buffers, load)
        for copy in loads:
            copy.start()
        for copy, step in out_copies[j]:
            wait_sent(copy, step)
        for copy in weights:
            copy.wait()
        for copy in loads:
            copy.wait()

        def expert_step(step, carry, j=j):
            expert_rows(step, buffers, x_ref)
            both = mul(x_ref[...], up_v[...])
            gate = both[:, :hidden_width]
            hidden = (gate / (1.0 + jnp.exp(-gate)) * both[:, hidden_width:]).astype(BF16)
            expert_results(step, mul(hidden, down_v[...]), [ref.at[j] for ref in stages])
            return carry

        lax.fori_loop(0, 4, expert_step, 0)
        if j == 0:
            weights = weight_copies(1)
            for copy in weights:
                copy.start()
        stores = whole_copies([ref.at[j] for ref in stages], [ref.at[j] for ref in staged], store)
        for copy in stores:
            copy.start()
        for copy in stores:
            copy.wait()
        copies = []
        for step in ORDER:
            for part in range(3):
                copy = plane_copy(
                    staged[part].at[j, plane_index(part, across(part, *step))],
                    returned[part].at[j, plane_index(part, (0, 0, 0, 0))],
                    send_back.at[j], receive_back.at[j], part, step,
                )
                copy.start()
                copies.append((copy, step))
        back_copies.append(copies)

    scatters = line_copies(lines, sums, scatter_semaphores, True)
    own, others = scatters[0:3], scatters[3:]
    row = lax.broadcasted_iota(jnp.int32, (2 * ROWS, TOK), 0).astype(F32)
    for j in range(2):
        for copy, step in back_copies[j]:
            wait_arrived(copy, step)
        loads = whole_copies([ref.at[j] for ref in returned], buffers, load)
        for copy in loads:
            copy.start()
        for n, d in enumerate((1, 3, 2, 0)):
            for part in range(3):
                if n == 0:
                    loads[part].wait()
                width = buffers[part].shape[2]
                a = lax.rem(line_place(part) + d, 4)
                tile = pl.ds(pl.multiple_of(a // 2 * 16, 16), 16)
                shift = (a % 2 * ROWS).astype(F32)
                mine = slice(32 * j, 32 * j + 32)
                slots = slot_ref[part, a, mine] + shift
                give = jnp.where(slots[:, None, :] == row, share_ref[part, a, mine][:, None, :], 0.0)
                high, low = halves(give.reshape(64 * ROWS, TOK))
                values = buffers[part][:, tile].reshape(64 * ROWS, width)
                both = mul(jnp.concatenate([high, low], axis=1), values, TN)
                if j == 0:
                    totals[part][a] = both[:TOK] + both[TOK:]
                else:
                    lines[part][a] = (totals[part][a] + both[:TOK] + both[TOK:]).astype(BF16)
                    copy = own[part] if d == 0 else others[3 * n + part]
                    copy.start()
    for part, (low, high) in enumerate(PARTS):
        for n in range(3):
            others[3 * n + part].wait()
        own[part].wait()
        total = mid_ref[:, low:high]
        for a in range(4):
            total = total + sums[part][a].astype(F32)
        out_ref[:, low:high] = total.astype(BF16)
    for copies in back_copies:
        for copy, step in copies:
            wait_sent(copy, step)


def moe(tables, mid, rows, up, down, top):
    dma = pltpu.SemaphoreType.DMA
    widths = [part.shape[1] for part in rows]
    exchange = [jax.ShapeDtypeStruct((2, 32, 4 * ROWS, width), BF16) for width in widths]
    return pl.pallas_call(
        functools.partial(moe_kernel, top),
        in_specs=[pl.BlockSpec(memory_space=pltpu.VMEM)] * 5 + [pl.BlockSpec(memory_space=pl.ANY)] * 2,
        out_specs=[pl.BlockSpec(memory_space=pltpu.VMEM)] + [pl.BlockSpec(memory_space=pl.ANY)] * 9,
        out_shape=[jax.ShapeDtypeStruct(mid.shape, BF16)] + exchange * 3,
        scratch_shapes=[pltpu.VMEM((4, TOK, width), BF16) for width in widths]
        + [pltpu.VMEM((2, 32, 4 * ROWS, width), BF16) for width in widths]
        + [pltpu.VMEM((32, 4 * ROWS, width), BF16) for width in widths]
        + [pltpu.VMEM((4, TOK, width), BF16) for width in widths]
        + [pltpu.VMEM((4, TOK, width), F32) for width in widths]
        + [pltpu.VMEM(up.shape[1:], BF16), pltpu.VMEM(down.shape[1:], BF16), pltpu.VMEM((256, up.shape[1]), BF16)]
        + [pltpu.VMEM((3, 4, 64, TOK), F32)] * 2
        + [dma((3, 4)), dma((3, 4)), dma((3,))] * 2
        + [dma((2, 3, 32))] * 4
        + [dma((3,)), dma((2,)), dma((3,))],
        compiler_params=pltpu.CompilerParams(
            collective_id=1, has_side_effects=True, vmem_limit_bytes=VMEM
        ),
        name="moe",
    )(tables, mid, *rows, up, down)[0]


def shards(
    query_rows,
    key_rows,
    value_rows,
    gate_z,
    log_decay,
    write_strength,
    norm_gain,
    out_weight,
    residual,
    post_gain,
    expert_ids,
    gate_scores,
    expert_up,
    expert_down,
):
    mid, rows_a, rows_b, rows_c, tables = mixer(
        query_rows[0], key_rows[0], value_rows[0], log_decay[0], write_strength[0], gate_z[0], norm_gain,
        residual[0], post_gain, jnp.transpose(expert_ids, (2, 0, 1)), jnp.transpose(gate_scores, (2, 0, 1)),
        out_weight, lax.axis_size("seq"),
    )
    rows = [rows_a, rows_b, rows_c]
    return moe(tables, mid, rows, expert_up, expert_down, expert_ids.shape[2])[None]


def solution(mesh):
    return jax.shard_map(
        shards,
        mesh=mesh,
        in_specs=(
            P("batch", "seq", None),
            P("batch", "seq", None),
            P("batch", "seq", None),
            P("batch", "seq", None),
            P("batch", None, "seq"),
            P("batch", None, "seq"),
            P(),
            P(),
            P("batch", "seq", None),
            P(),
            P("batch", "seq", None),
            P("batch", "seq", None),
            P(("seq", "batch"), None, None),
            P(("seq", "batch"), None, None),
        ),
        out_specs=P("batch", "seq", None),
        check_vma=False,
    )
```

time: 238 us -> 216 us (0.908)
  Pallas kernels: 230 us -> 213 us
  other arithmetic: 5.06 us -> 0 us
    pallas_call x4 -> x2, Pallas kernels: 230 us -> 213 us  [the longest x1 174 us: moe(): pl.pallas_call(functools.partial(moe_kernel, top), in_specs=[pl.BlockSpec...]
where the time goes in v5:
time: 216 us; the launch traced here: 215 us
  Pallas kernels  213 us (99%)
    pallas_call x1, Pallas kernels, moe(): pl.pallas_call(functools.partial(moe_kernel, top), in_specs=[pl.BlockSpec...  174 us
    pallas_call x1, Pallas kernels, mixer(): pl.pallas_call(mixer_kernel, in_specs=[pl.BlockSpec(memory_space=vmem)] *...  39.1 us

profile of v5, /device:TPU:1, one launch (start us, length us, event | category | flops | bytes accessed | tf_op | source)
XLA Modules:
  0.0 215.3 jit_solution(2302907615609628637)
XLA Ops:
  0.0 39.1 %mixer.1 = (f32[128,2048]{1,0:T(8,128)}, bf16[128,768]{1,0:T(8,128)(2,1)}, bf16[128,640]{1,0:T(8,128)(2,1)}, bf16[128,640]{1,0:T(8,128)(2,1)}, bf16[3,4,48,128]{3,2,1,0:T(8,128)(2,1)}) custom-call(bf16[128,1024]{1,0:T(8,128)(2,1)} %bitcast.16, bf16[128,1024]{1,0:T(8,128)(2,1)} %bitcast.17, bf16[128,2048]{1,0:T(8,128)(2,1)} %bitcast.12, ...), custom_call_target="tpu_custom_call" | custom-call | tf_op jit(solution)/shard_map/mixer/pallas_call | solution.py:325
  39.1 174.3 %moe.1 = (bf16[128,2048]{1,0:T(8,128)(2,1)}, bf16[2,32,32,768]{3,2,1,0:T(8,128)(2,1)}, bf16[2,32,32,640]{3,2,1,0:T(8,128)(2,1)}, bf16[2,32,32,640]{3,2,1,0:T(8,1...) custom-call(bf16[3,4,48,128]{3,2,1,0:T(8,128)(2,1)} %get-tuple-eleme, ...), custom_call_target="tpu_custom_call" | custom-call | tf_op jit(solution)/shard_map/moe/pallas_call | solution.py:638
  213.4 1.9 copy.16

commit v6 on v5

--- a/solution.py
+++ b/solution.py
@@ -254,7 +254,6 @@
     @pl.when(core == 0)
     def _():
         def step(place, state):
-            pltpu.make_async_copy(inbox.at[place], inbox.at[place], receive.at[place]).wait()
             high, low = halves(state)
             outbox[place] = high
 
@@ -271,7 +270,15 @@
             gamma = parts[0:1] + parts[1:2] + parts[2:3]
             return state * gamma + (both[:DK] + both[DK:]) + inbox[place, 128:256].astype(F32)
 
-        lax.fori_loop(0, count, step, jnp.zeros((DK, DK), F32))
+        def steps(group, state):
+            for n in range(4):
+                place = group * 4 + n
+                pltpu.make_async_copy(inbox.at[place], inbox.at[place], receive.at[place]).wait()
+            for n in range(4):
+                state = step(group * 4 + n, state)
+            return state
+
+        lax.fori_loop(0, count // 4, steps, jnp.zeros((DK, DK), F32))
 
     for h in range(HV):
         pltpu.make_async_copy(state_ref.at[h], state_ref.at[h], receive_back.at[h]).wait()
@@ -482,9 +489,9 @@
     tables_ref, mid_ref, rows, up_ref, down_ref = refs[0], refs[1], refs[2:5], refs[5], refs[6]
     out_ref, arrived, returned, staged = refs[7], refs[8:11], refs[11:14], refs[14:17]
     lines, stages, buffers, sums, totals = refs[17:20], refs[20:23], refs[23:26], refs[26:29], refs[29:32]
-    up_v, down_v, x_ref, slot_ref, share_ref = refs[32:37]
-    gather_semaphores, scatter_semaphores = refs[37:40], refs[40:43]
-    send, receive, send_back, receive_back, load, fetch, store = refs[43:50]
+    up_v, down_v, x_ref, slot_ref, share_ref, take_ref = refs[32:38]
+    gather_semaphores, scatter_semaphores = refs[38:41], refs[41:44]
+    send, receive, send_back, receive_back, load, fetch, store = refs[44:51]
     hidden_width = down_ref.shape[1]
 
     def weight_copies(j):
@@ -501,6 +508,20 @@
     for copy in gathers:
         copy.start()
     fill_slots(tables_ref, slot_ref, share_ref, top)
+    for j in range(2):
+        for g in range(2):
+            for part in range(3):
+                places = [plane_index(part, across(part, *step)) for step in ORDER[16 * g:16 * g + 16]]
+
+                def ready(a, carry, part=part, places=places, g=g, j=j):
+                    slots = jnp.concatenate(
+                        [slot_ref[part, a, pl.ds(place + 32 * j, 1)] for place in places], axis=0
+                    )
+                    take = jnp.where(picked(slots), 1.0, 0.0).reshape(16 * ROWS, TOK).astype(BF16)
+                    take_ref[(part * 2 + j) * 2 + g, a] = take
+                    return carry
+
+                lax.fori_loop(0, 4, ready, 0)
     for copy in gathers:
         copy.wait()
 
@@ -512,16 +533,12 @@
             group = slice(16 * g, 16 * g + 16)
             stores = []
             for part in range(3):
-                places = [plane_index(part, across(part, *step)) for step in steps]
-
-                def fill(pair, carry, part=part, places=places, group=group, j=j):
+
+                def fill(pair, carry, part=part, group=group, g=g, j=j):
                     packed = []
                     for n in range(2):
                         a = pair * 2 + n
-                        slots = jnp.concatenate(
-                            [slot_ref[part, a, pl.ds(place + 32 * j, 1)] for place in places], axis=0
-                        )
-                        take = jnp.where(picked(slots), 1.0, 0.0).reshape(16 * ROWS, TOK).astype(BF16)
+                        take = take_ref[(part * 2 + j) * 2 + g, a]
                         packed.append(mul(take, lines[part][a]).reshape(16, ROWS, lines[part].shape[2]))
                     tile = pl.ds(pl.multiple_of(pair * 16, 16), 16)
                     stages[part][j, group, tile] = jnp.concatenate(packed, axis=1).astype(BF16)
@@ -598,9 +615,9 @@
         loads = whole_copies([ref.at[j] for ref in returned], buffers, load)
         for copy in loads:
             copy.start()
-        for n, d in enumerate((1, 3, 2, 0)):
+        for d in (2, 1, 3, 0):
             for part in range(3):
-                if n == 0:
+                if d == 2:
                     loads[part].wait()
                 width = buffers[part].shape[2]
                 a = lax.rem(line_place(part) + d, 4)
@@ -616,7 +633,7 @@
                     totals[part][a] = both[:TOK] + both[TOK:]
                 else:
                     lines[part][a] = (totals[part][a] + both[:TOK] + both[TOK:]).astype(BF16)
-                    copy = own[part] if d == 0 else others[3 * n + part]
+                    copy = own[part] if d == 0 else others[3 * (0, 0, 2, 1)[d] + part]
                     copy.start()
     for part, (low, high) in enumerate(PARTS):
         for n in range(3):
@@ -646,7 +663,7 @@
         + [pltpu.VMEM((4, TOK, width), BF16) for width in widths]
         + [pltpu.VMEM((4, TOK, width), F32) for width in widths]
         + [pltpu.VMEM(up.shape[1:], BF16), pltpu.VMEM(down.shape[1:], BF16), pltpu.VMEM((256, up.shape[1]), BF16)]
-        + [pltpu.VMEM((3, 4, 64, TOK), F32)] * 2
+        + [pltpu.VMEM((3, 4, 64, TOK), F32)] * 2 + [pltpu.VMEM((12, 4, 16 * ROWS, TOK), BF16)]
         + [dma((3, 4)), dma((3, 4)), dma((3,))] * 2
         + [dma((2, 3, 32))] * 4
         + [dma((3,)), dma((2,)), dma((3,))],

time: 216 us -> 215 us (level)
  no operation moved by 1% of the time
where the time goes in v6:
time: 215 us
  Pallas kernels  213 us (99%)
    pallas_call x1, Pallas kernels, moe(): pl.pallas_call(functools.partial(moe_kernel, top), in_specs=[pl.BlockSpec...  173 us
    pallas_call x1, Pallas kernels, mixer(): pl.pallas_call(mixer_kernel, in_specs=[pl.BlockSpec(memory_space=vmem)] *...  39.7 us

profile of v6, /device:TPU:1, one launch (start us, length us, event | category | flops | bytes accessed | tf_op | source)
XLA Modules:
  0.0 214.9 jit_solution(5937304574030296403)
XLA Ops:
  0.0 39.7 %mixer.1 = (f32[128,2048]{1,0:T(8,128)}, bf16[128,768]{1,0:T(8,128)(2,1)}, bf16[128,640]{1,0:T(8,128)(2,1)}, bf16[128,640]{1,0:T(8,128)(2,1)}, bf16[3,4,48,128]{3,2,1,0:T(8,128)(2,1)}) custom-call(bf16[128,1024]{1,0:T(8,128)(2,1)} %bitcast.16, bf16[128,1024]{1,0:T(8,128)(2,1)} %bitcast.17, bf16[128,2048]{1,0:T(8,128)(2,1)} %bitcast.12, ...), custom_call_target="tpu_custom_call" | custom-call | tf_op jit(solution)/shard_map/mixer/pallas_call | solution.py:332
  39.7 173.3 %moe.1 = (bf16[128,2048]{1,0:T(8,128)(2,1)}, bf16[2,32,32,768]{3,2,1,0:T(8,128)(2,1)}, bf16[2,32,32,640]{3,2,1,0:T(8,128)(2,1)}, bf16[2,32,32,640]{3,2,1,0:T(8,1...) custom-call(bf16[3,4,48,128]{3,2,1,0:T(8,128)(2,1)} %get-tuple-eleme, ...), custom_call_target="tpu_custom_call" | custom-call | tf_op jit(solution)/shard_map/moe/pallas_call | solution.py:655
  213.0 1.9 copy.16
